TPU v7x, 128 devices: a whole 4x4x4 slice. The times are simulated.
128 devices in a mesh: wide: 16 (over y, x_lo, core), narrow: 8 (over x_hi, z).
Axes of the slice: x: 4 (x_hi: 2, x_lo: 2; x = x_hi * 2 + x_lo), y: 4, z: 4, core: 2. Of those that a mesh axis runs over, the one named last changes fastest.
Arguments:
- state: float32 [5, 2048, 4, 4096], P(None, ('wide', 'narrow')), may hold values from -3.75 to 46, as said below
Outputs:
- advanced: float32 [5, 2048, 4, 4096], P(None, ('wide', 'narrow'))
Inputs may be any that keep to these rules, and one draw needn't show every extreme that they name: state holds density in [0.5, 2.5], momenta, and total energy whose pressure (gamma 1.4) lies in [0.4, 15].
All inputs are finite; a program needn't handle non-finite values. Where the computation divides by a largest or mean magnitude, that divisor is 1e-20 or more.
Results may differ from a plain program's by a relative error of at most 0.0003.
Values sent between devices are 32-bit elements; how exact they have to be, the bound alone decides.
No kernel may reach another device: no remote copies, remote signals or barrier semaphores. Data moves between devices by JAX's collectives and lax.ppermute only.
A program may use at most 128 MiB of HBM per device.

v0:
```python
import jax
import jax.numpy as jnp
from jax import lax
from jax.sharding import Mesh
from jax.sharding import PartitionSpec as P

WIDE_NARROW = ("wide_0", "wide_1", "wide_2", "narrow_0", "narrow_1")


gamma_minus = 0.4
gamma_ratio = 1.4
courant_number = 0.6


def one_axis_at_a_time(array, axes):
    for axis in axes:
        array = lax.pmax(array, axis)
    return array


def with_halo(array, sides, width):
    edges = {}
    for axis, dim in sides:
        count, length = (lax.axis_size(axis), array.shape[dim])
        up = [(i, (i + 1) % count) for i in range(count)]
        last = lax.slice_in_dim(array, length - width, length, axis=dim)
        first = lax.slice_in_dim(array, 0, width, axis=dim)
        edges[dim] = (
            lax.ppermute(last, axis, up),
            lax.ppermute(first, axis, [(b, a) for a, b in up]),
        )
    done = []
    for _, dim in sides:
        low, high = edges[dim]
        around = [(width, width) if d in done else (0, 0) for d in range(array.ndim)]
        array = jnp.concatenate([jnp.pad(low, around), array, jnp.pad(high, around)], axis=dim)
        done.append(dim)
    return array


def primitives(cons_vars):
    density = cons_vars[0]
    velocity = cons_vars[1:4] / density
    pressure = gamma_minus * (cons_vars[4] - 0.5 * density * jnp.sum(velocity * velocity, axis=0))
    return jnp.concatenate([density[None], velocity, pressure[None]], 0)


def euler_flux(prim_vars, normal):
    density = prim_vars[0]
    velocity = prim_vars[1:4]
    pressure = prim_vars[4]
    normal_speed = prim_vars[normal]
    momentum = density * velocity
    energy = pressure / gamma_minus + 0.5 * density * jnp.sum(velocity * velocity, axis=0)
    cons_vars = jnp.concatenate([density[None], momentum, energy[None]], 0)
    components = [
        momentum[entry] * normal_speed + (pressure if entry == normal - 1 else 0.0)
        for entry in range(3)
    ]
    fluxes = jnp.stack(
        [density * normal_speed] + components + [(energy + pressure) * normal_speed], 0
    )
    signal = jnp.abs(normal_speed) + jnp.sqrt(gamma_ratio * pressure / density)
    return (cons_vars, fluxes, signal)


def ppm_sweep(padded, sweep_axis, normal, time_step):
    length = padded.shape[sweep_axis]

    def take_slice(values, start, limit):
        return lax.slice_in_dim(values, start, limit, axis=sweep_axis)

    prim_vars = primitives(padded)
    jumps = take_slice(prim_vars, 1, length) - take_slice(prim_vars, 0, length - 1)
    back_jump = take_slice(jumps, 0, length - 2)
    fore_jump = take_slice(jumps, 1, length - 1)
    centred = 0.5 * (back_jump + fore_jump)
    magnitude = jnp.minimum(
        jnp.abs(centred), 2.0 * jnp.minimum(jnp.abs(back_jump), jnp.abs(fore_jump))
    )
    slopes = jnp.where(back_jump * fore_jump > 0, jnp.sign(centred) * magnitude, 0.0)
    faces = (
        0.5 * (take_slice(prim_vars, 1, length - 2) + take_slice(prim_vars, 2, length - 1))
        - (take_slice(slopes, 1, length - 2) - take_slice(slopes, 0, length - 3)) / 6.0
    )
    centre = take_slice(prim_vars, 2, length - 2)
    left_edge = take_slice(faces, 0, length - 4)
    right_edge = take_slice(faces, 1, length - 3)
    flatten = (right_edge - centre) * (centre - left_edge) <= 0
    edge_gap = right_edge - left_edge
    offset = centre - 0.5 * (left_edge + right_edge)
    left_new = jnp.where(
        edge_gap * offset > edge_gap * edge_gap / 6.0, 3.0 * centre - 2.0 * right_edge, left_edge
    )
    right_new = jnp.where(
        -edge_gap * edge_gap / 6.0 > edge_gap * offset, 3.0 * centre - 2.0 * left_edge, right_edge
    )
    left_edge = jnp.where(flatten, centre, left_new)
    right_edge = jnp.where(flatten, centre, right_new)
    courant = (
        time_step * (jnp.abs(centre[normal]) + jnp.sqrt(gamma_ratio * centre[4] / centre[0]))[None]
    )
    edge_gap = right_edge - left_edge
    curvature = 6.0 * (centre - 0.5 * (left_edge + right_edge))
    shrink = 1.0 - 2.0 * courant / 3.0
    to_right = right_edge - 0.5 * courant * (edge_gap - shrink * curvature)
    to_left = left_edge + 0.5 * courant * (edge_gap + shrink * curvature)
    left_cons, left_flux, left_speed = euler_flux(take_slice(to_right, 0, length - 5), normal)
    right_cons, right_flux, right_speed = euler_flux(take_slice(to_left, 1, length - 4), normal)
    fluxes = 0.5 * (left_flux + right_flux) - 0.5 * jnp.maximum(left_speed, right_speed)[None] * (
        right_cons - left_cons
    )
    interior = take_slice(padded, 3, length - 3)
    return interior - time_step * (
        take_slice(fluxes, 1, length - 5) - take_slice(fluxes, 0, length - 6)
    )


def wrap_pad(values, sweep_axis):
    extent = values.shape[sweep_axis]
    return jnp.concatenate(
        [
            lax.slice_in_dim(values, extent - 3, extent, axis=sweep_axis),
            values,
            lax.slice_in_dim(values, 0, 3, axis=sweep_axis),
        ],
        sweep_axis,
    )


def local(state):
    prim_vars = primitives(state)
    sound = jnp.sqrt(gamma_ratio * prim_vars[4] / prim_vars[0])
    local_peak = jnp.max(jnp.maximum(jnp.abs(prim_vars[1]), jnp.abs(prim_vars[2])) + sound)
    peak_speed = one_axis_at_a_time(local_peak, WIDE_NARROW)
    time_step = courant_number / peak_speed
    state = ppm_sweep(wrap_pad(state, 3), 3, 1, 0.5 * time_step)
    padded = with_halo(state, ((WIDE_NARROW, 1),), 3)
    state = ppm_sweep(padded, 1, 2, time_step)
    state = ppm_sweep(wrap_pad(state, 3), 3, 1, 0.5 * time_step)
    return state


def solution(mesh):
    split = Mesh(
        mesh.devices.reshape(4, 2, 2, 2, 4), ("wide_0", "wide_1", "wide_2", "narrow_0", "narrow_1")
    )
    placed = (P(None, WIDE_NARROW, None, None),)
    return jax.shard_map(
        local,
        mesh=split,
        in_specs=placed,
        out_specs=P(None, WIDE_NARROW, None, None),
        check_vma=False,
    )
```

profile of v0, /device:TPU:0, one launch (start us, length us, event | category | flops | bytes accessed | tf_op | source)
XLA Modules:
  0.0 384.7 jit_solution(6350360623617297098)
XLA Ops:
  8.6 11.4 %pmax.35 = f32[]{:T(128)} all-reduce(f32[]{:T(128)} %fusion.69), channel_id=1, replica_groups=mesh['wide_0'=4,'wide_1'=2,'wide_2'=2,'narrow_0'=2,'narrow_1'=4] {'wide_0'}, use_global_device_ids=true, to_apply=%region_2.0 | all-reduce | flops 1 | bytes 8 | tf_op jit(solution)/shard_map/pmax | solution.py:17
  20.0 5.5 %pmax.36 = f32[]{:T(128)} all-reduce(f32[]{:T(128)} %pmax.35), channel_id=1, replica_groups=mesh['wide_0'=4,'wide_1'=2,'wide_2'=2,'narrow_0'=2,'narrow_1'=4] {'wide_1'}, use_global_device_ids=true, to_apply=%region_3.0 | all-reduce | flops 1 | bytes 8 | tf_op jit(solution)/shard_map/pmax | solution.py:17
  28.7 7.1 %pmax.38 = f32[]{:T(128)} all-reduce(f32[]{:T(128)} %pmax.37), channel_id=1, replica_groups=mesh['wide_0'=4,'wide_1'=2,'wide_2'=2,'narrow_0'=2,'narrow_1'=4] {'narro..., use_global_device_ids=true, to_apply=%region_5.0 | all-reduce | flops 1 | bytes 8 | tf_op jit(solution)/shard_map/pmax | solution.py:17
  36.9 12.6 %pmax.39 = f32[]{:T(128)} all-reduce(f32[]{:T(128)} %pmax.38), channel_id=1, replica_groups=mesh['wide_0'=4,'wide_1'=2,'wide_2'=2,'narrow_0'=2,'narrow_1'=4] {'narro..., use_global_device_ids=true, to_apply=%region_6.0 | all-reduce | flops 1 | bytes 8 | tf_op jit(solution)/shard_map/pmax | solution.py:17
  49.5 11.1 %concatenate.36 = f32[5,16,4,4102]{3,2,1,0:T(4,128)} concatenate(f32[5,16,4,3]{3,2,1,0:T(4,128)S(1)} %get-tuple-element.88, f32[5,16,4,4096]{3,2,1,0:T(4,128)} %param.1, f32[5,16,4,3]{3,2,1,0:T(4,128)S(1)} %get-tuple-element.87), dimensions={3} | concatenate | bytes 10501120 | tf_op jit(solution)/shard_map/concatenate | solution.py:121
  79.2 7.2 %multiply_select_fusion.2 = f32[5,16,4,4100]{3,2,1,0:T(4,128)S(1)} fusion(f32[5,16,4,4101]{3,2,1,0:T(4,128)S(1)} %slice_subtract_fusion.5), kind=kLoop, calls=%fused_computation.68 | loop fusion | flops 17056000 | bytes 15744000 | tf_op jit(solution)/shard_map/jit(_where)/select_n | solution.py:81
  86.4 9.1 %fusion.15 = f32[5,16,4,4099]{3,2,1,0:T(4,128)S(1)} fusion(f32[5,16,4,4100]{3,2,1,0:T(4,128)S(1)} %multiply_select_fusion.2, f32[5,16,4,4102]{3,2,1,0:T(4,128)S(1)} %pad_maximum_fusion.2), kind=kLoop, calls=%fused_computation.38 | loop fusion | flops 6558400 | bytes 26233600 | tf_op jit(solution)/shard_map/sub | solution.py:83
  95.5 12.9 %multiply_subtract_fusion.2 = (f32[5,16,4,4098]{3,2,1,0:T(4,128)S(1)}, f32[5,16,4,4098]{3,2,1,0:T(4,128)S(1)}, f32[5,16,4,4098]{3,2,1,0:T(4,128)S(1)}) fusion(f32[16,4,4098]{2,1,0:T(4,128)S(1)} %multiply_bitcast_fusion.8, f32[16,4,4098]{2,1,0:T(4,128)S(1)} %copy-done.1, f32[5,16,4,4102]{3,2,1,0:T(4,128)S(1)} %pad_maximum_fusion.2, ...), kind=kLoop, calls=%fused_computation.61 | loop fusion | flops 43274880 | bytes 33570816 | tf_op jit(solution)/shard_map/sub | solution.py:106
  138.6 11.9 %fusion.26 = f32[5,16,4,4096]{3,2,1,0:T(4,128)} fusion(f32[5,16,4,4096]{3,2,1,0:T(4,128)} %param.1, f32[5,16,4,4097]{3,2,1,0:T(4,128)} %fusion.18, f32[]{:T(128)S(6)} %mul.752), kind=kLoop, calls=%fused_computation.78 | loop fusion | flops 3932160 | bytes 20971524 | tf_op jit(solution)/shard_map/sub | solution.py:114
  152.4 7.2 %collective-permute-start.1 = (f32[5,3,4,4096]{3,2,1,0:T(4,128)S(1)}, f32[5,3,4,4096]{3,2,1,0:T(4,128)S(1)}, u32[]{:S(2)}, u32[]{:S(2)}) collective-permute-start(f32[5,3,4,4096]{3,2,1,0:T(4,128)S(1)} %get-tuple-element.86), channel_id=1, source_target_pairs={{1,0},{2,1},{3,2},{4,3},{5,4},{6,5},{7,6},{8,7},{9,8},{10,9},{11,1... | collective-permute-start | bytes 2949128 | tf_op jit(solution)/shard_map/ppermute | solution.py:30
  159.5 17.8 %collective-permute-done = f32[5,3,4,4096]{3,2,1,0:T(4,128)S(1)} collective-permute-done((f32[5,3,4,4096]{3,2,1,0:T(4,128)S(1)}, f32[5,3,4,4096]{3,2,1,0:T(4,128)S(1)}, u32[]{:S(2)}, u32[]{:S(2)}) %collective-permute-start) | collective-permute-done | bytes 983072 | tf_op jit(solution)/shard_map/ppermute | solution.py:29
  186.7 8.6 %pad_maximum_fusion.1 = f32[5,22,4,4096]{3,2,1,0:T(4,128)} fusion(f32[1,22,4,4096]{3,2,1,0:T(4,128)} %fusion.27, f32[3,22,4,4096]{3,2,1,0:T(4,128)} %get-tuple-element.26, f32[1,22,4,4096]{3,2,1,0:T(4,128)S(1)} %pad_maximum_fusion.4), kind=kLoop, calls=%fused_computation.4 | loop fusion | flops 3604480 | bytes 14417920 | tf_op jit(solution)/shard_map/concatenate | solution.py:45
  199.7 12.0 %slice_subtract_fusion = f32[5,21,4,4096]{3,2,1,0:T(4,128)} fusion(f32[5,22,4,4096]{3,2,1,0:T(4,128)} %pad_maximum_fusion.1), kind=kLoop, calls=%fused_computation.5 | loop fusion | flops 1720320 | bytes 20643840 | tf_op jit(solution)/shard_map/sub | solution.py:74
  211.7 10.2 %multiply_select_fusion = f32[5,20,4,4096]{3,2,1,0:T(4,128)S(1)} fusion(f32[5,21,4,4096]{3,2,1,0:T(4,128)} %slice_subtract_fusion), kind=kLoop, calls=%fused_computation.6 | loop fusion | flops 21299200 | bytes 19660800 | tf_op jit(solution)/shard_map/jit(_where)/select_n | solution.py:81
  221.9 8.3 %fusion.1 = f32[5,19,4,4096]{3,2,1,0:T(4,128)S(1)} fusion(f32[5,20,4,4096]{3,2,1,0:T(4,128)S(1)} %multiply_select_fusion, f32[5,22,4,4096]{3,2,1,0:T(4,128)} %pad_maximum_fusion.1), kind=kLoop, calls=%fused_computation.10 | loop fusion | flops 7782400 | bytes 31129600 | tf_op jit(solution)/shard_map/sub | solution.py:83
  230.3 13.6 %multiply_subtract_fusion = (f32[5,18,4,4096]{3,2,1,0:T(4,128)S(1)}, f32[5,18,4,4096]{3,2,1,0:T(4,128)S(1)}, f32[5,18,4,4096]{3,2,1,0:T(4,128)}) fusion(f32[18,4,4096]{2,1,0:T(4,128)S(1)} %copy-done, f32[18,4,4096]{2,1,0:T(4,128)S(1)} %get-tuple-element.23, f32[5,22,4,4096]{3,2,1,0:T(4,128)S(1)} %bitcast.96, f32[5,19,4,4096]{3,2,1,0:T(4,128)S(1)} %fusion.1), kind=kLoop, calls=%fused_computation.16 | loop fusion | flops 48660480 | bytes 37748736 | tf_op jit(solution)/shard_map/sub | solution.py:106
  243.9 6.1 %multiply_add_fusion = f32[5,18,4,4096]{3,2,1,0:T(4,128)S(1)} fusion(f32[5,18,4,4096]{3,2,1,0:T(4,128)} %get-tuple-element.22, f32[18,4,4096]{2,1,0:T(4,128)} %multiply_bitcast_fusion.1, f32[5,18,4,4096]{3,2,1,0:T(4,128)S(1)} %get-tuple-element.21, f32[18,4,4096]{2,1,0:T(4,128)S(1)} %get-tuple-element.23, f32[5,22,4,4096]{3,2,1,0:T(4,128)S(1)} %bitcast.96), kind=kLoop, calls=%fused_computation.15 | loop fusion | flops 11796480 | bytes 25952256 | tf_op jit(solution)/shard_map/add | solution.py:107
  269.9 7.4 %fusion.6 = f32[5,17,4,4096]{3,2,1,0:T(4,128)} fusion(f32[1,17,4,4096]{3,2,1,0:T(4,128)S(1)} %get-tuple-element.17, f32[3,17,4,4096]{3,2,1,0:T(4,128)S(1)} %get-tuple-element.50, f32[1,17,4,4096]{3,2,1,0:T(4,128)S(1)} %get-tuple-element.44, f32[1,17,4,4096]{3,2,1,0:T(4,128)S(1)} %get-tuple-element.19, f32[3,17,4,4096]{3,2,1,0:T(4,128)S(1)} %get-tuple-element.46, ...), kind=kLoop, calls=%fused_computation.25 | loop fusion | flops 12533760 | bytes 28966912 | tf_op jit(solution)/shard_map/sub | solution.py:110
  277.2 12.5 %fusion.24 = f32[5,16,4,4096]{3,2,1,0:T(4,128)} fusion(f32[5,16,4,4096]{3,2,1,0:T(4,128)} %fusion.26, f32[5,17,4,4096]{3,2,1,0:T(4,128)} %fusion.6, f32[]{:T(128)S(6)} %div.151), kind=kLoop, calls=%fused_computation.75 | loop fusion | flops 3932160 | bytes 20971524 | tf_op jit(solution)/shard_map/sub | solution.py:114
  290.9 11.5 %concatenate.44 = f32[5,16,4,4102]{3,2,1,0:T(4,128)} concatenate(f32[5,16,4,3]{3,2,1,0:T(4,128)S(1)} %get-tuple-element.84, f32[5,16,4,4096]{3,2,1,0:T(4,128)} %fusion.24, f32[5,16,4,3]{3,2,1,0:T(4,128)S(1)} %get-tuple-element.83), dimensions={3} | concatenate | bytes 10501120 | tf_op jit(solution)/shard_map/concatenate | solution.py:121
  314.5 7.2 %multiply_select_fusion.1 = f32[5,16,4,4100]{3,2,1,0:T(4,128)S(1)} fusion(f32[5,16,4,4101]{3,2,1,0:T(4,128)S(1)} %slice_subtract_fusion.3), kind=kLoop, calls=%fused_computation.58 | loop fusion | flops 17056000 | bytes 15744000 | tf_op jit(solution)/shard_map/jit(_where)/select_n | solution.py:81
  321.6 8.9 %fusion.12 = f32[5,16,4,4099]{3,2,1,0:T(4,128)S(1)} fusion(f32[5,16,4,4100]{3,2,1,0:T(4,128)S(1)} %multiply_select_fusion.1, f32[5,16,4,4102]{3,2,1,0:T(4,128)S(1)} %pad_maximum_fusion.3), kind=kLoop, calls=%fused_computation.32 | loop fusion | flops 6558400 | bytes 26233600 | tf_op jit(solution)/shard_map/sub | solution.py:83
  330.5 12.9 %multiply_subtract_fusion.1 = (f32[5,16,4,4098]{3,2,1,0:T(4,128)S(1)}, f32[5,16,4,4098]{3,2,1,0:T(4,128)S(1)}, f32[5,16,4,4098]{3,2,1,0:T(4,128)S(1)}) fusion(f32[16,4,4098]{2,1,0:T(4,128)S(1)} %multiply_bitcast_fusion.5, f32[16,4,4098]{2,1,0:T(4,128)S(1)} %get-tuple-element.12, f32[5,16,4,4102]{3,2,1,0:T(4,128)S(1)} %pad_maximum_fusion.3, ...), kind=kLoop, calls=%fused_computation.51 | loop fusion | flops 43274880 | bytes 33570816 | tf_op jit(solution)/shard_map/sub | solution.py:106
  372.7 11.8 %fusion.22 = f32[5,16,4,4096]{3,2,1,0:T(4,128)} fusion(f32[5,16,4,4096]{3,2,1,0:T(4,128)} %fusion.24, f32[5,16,4,4097]{3,2,1,0:T(4,128)} %fusion.20, f32[]{:T(128)S(6)} %mul.752), kind=kLoop, calls=%fused_computation.72 | loop fusion | flops 3932160 | bytes 20971524 | tf_op jit(solution)/shard_map/sub | solution.py:114
  (110 shorter events, 138.5 us)
Async XLA Ops:
  70.4 4.5 %copy-start.2 = (f32[1,16,4,4102]{3,2,1,0:T(4,128)S(1)}, f32[1,16,4,4102]{3,2,1,0:T(4,128)}, u32[]{:S(2)}) copy-start(f32[1,16,4,4102]{3,2,1,0:T(4,128)} %fusion.61) | copy-start | bytes 3150340
  70.4 4.4 %copy-start.8 = (f32[1,16,4,4102]{3,2,1,0:T(4,128)S(1)}, f32[1,16,4,4102]{3,2,1,0:T(4,128)}, u32[]{:S(2)}) copy-start(f32[1,16,4,4102]{3,2,1,0:T(4,128)} %get-tuple-element.81) | copy-start | bytes 3150340
  86.3 9.1 %copy-start.1 = (f32[16,4,4098]{2,1,0:T(4,128)S(1)}, f32[16,4,4098]{2,1,0:T(4,128)}, u32[]{:S(2)}) copy-start(f32[16,4,4098]{2,1,0:T(4,128)} %get-tuple-element.34) | copy-start | bytes 3147268
  128.1 1.2 copy-start.5
  128.1 3.3 copy-start.6
  131.3 1.2 copy-start.9
  131.4 1.6 copy-start.10
  131.4 1.9 copy-start.11
  150.5 28.4 %slice-start.2 = ((s8[5242880]{0:T(1024)(128)(4,1)}), s8[4194304]{0:T(1024)(128)(4,1)S(1)}, s32[]{:S(2)}) async-start(s8[5242880]{0:T(1024)(128)(4,1)} %bitcast.97), calls=%async_computation.2 | async-start | bytes 8388608
  152.3 25.0 %collective-permute-start = (f32[5,3,4,4096]{3,2,1,0:T(4,128)S(1)}, f32[5,3,4,4096]{3,2,1,0:T(4,128)S(1)}, u32[]{:S(2)}, u32[]{:S(2)}) collective-permute-start(f32[5,3,4,4096]{3,2,1,0:T(4,128)S(1)} %get-tuple-element.85), channel_id=1, source_target_pairs={{0,1},{1,2},{2,3},{3,4},{4,5},{5,6},{6,7},{7,8},{8,9},{9,10},{10,1... | collective-permute-start | bytes 2949128 | tf_op jit(solution)/shard_map/ppermute | solution.py:29
  152.4 26.5 %slice-start.3 = ((s8[5242880]{0:T(1024)(128)(4,1)}), s8[1048576]{0:T(1024)(128)(4,1)S(1)}, s32[]{:S(2)}) async-start(s8[5242880]{0:T(1024)(128)(4,1)} %bitcast.97), calls=%async_computation.3 | async-start | bytes 2097152
  152.4 24.9 %collective-permute-start.1 = (f32[5,3,4,4096]{3,2,1,0:T(4,128)S(1)}, f32[5,3,4,4096]{3,2,1,0:T(4,128)S(1)}, u32[]{:S(2)}, u32[]{:S(2)}) collective-permute-start(f32[5,3,4,4096]{3,2,1,0:T(4,128)S(1)} %get-tuple-element.86), channel_id=1, source_target_pairs={{1,0},{2,1},{3,2},{4,3},{5,4},{6,5},{7,6},{8,7},{9,8},{10,9},{11,1... | collective-permute-start | bytes 2949128 | tf_op jit(solution)/shard_map/ppermute | solution.py:30
  211.7 18.6 %slice-start = ((s8[7208960]{0:T(1024)(128)(4,1)}), s8[4194304]{0:T(1024)(128)(4,1)S(1)}, s32[]{:S(2)}) async-start(s8[7208960]{0:T(1024)(128)(4,1)} %bitcast.95), calls=%async_computation | async-start | bytes 8388608
  221.9 8.4 %slice-start.1 = ((s8[7208960]{0:T(1024)(128)(4,1)}), s8[3014656]{0:T(1024)(128)(4,1)S(1)}, s32[]{:S(2)}) async-start(s8[7208960]{0:T(1024)(128)(4,1)} %bitcast.95), calls=%async_computation.1 | async-start | bytes 6029312
  221.9 8.4 %copy-start = (f32[18,4,4096]{2,1,0:T(4,128)S(1)}, f32[18,4,4096]{2,1,0:T(4,128)}, u32[]{:S(2)}) copy-start(f32[18,4,4096]{2,1,0:T(4,128)} %multiply_bitcast_fusion.1) | copy-start | bytes 3538948
  264.8 2.6 copy-start.3
  302.5 5.3 %slice-start.4 = ((s8[5406720]{0:T(1024)(128)(4,1)}), s8[4194304]{0:T(1024)(128)(4,1)S(1)}, s32[]{:S(2)}) async-start(s8[5406720]{0:T(1024)(128)(4,1)} %bitcast.99), calls=%async_computation.4 | async-start | bytes 8388608
  304.1 3.6 slice-start.5
  363.1 1.2 copy-start.7
  363.5 1.7 copy-start.4
  365.1 2.1 copy-start.12
  365.2 2.1 copy-start.13
  365.2 2.1 copy-start.14
where the time goes:
time: 390 us; the launch traced here: 385 us
  other arithmetic  283 us (73%)
  blocking collectives  39.7 us (10%)
  local copies, waits for them, and re-layouts  35.2 us (9%)
  waiting for transfers between devices  17.8 us (5%)
  starting transfers between devices  7.23 us (2%)
    pmax x5, blocking collectives, one_axis_at_a_time(): array = lax.pmax(array, axis)  39.7 us
    sub x3, other arithmetic, ppm_sweep(): to_right = right_edge - 0.5 * courant * (edge_gap - shrink * curvature)  39.5 us
    sub x3, other arithmetic, ppm_sweep(): interior - time_step * (take_slice(fluxes, 1, length - 5) - take_slice(fl...  36.2 us
    sub x3, other arithmetic, ppm_sweep(): 0.5 * (take_slice(prim_vars, 1, length - 2) + take_slice(prim_vars, 2, le...  26.3 us
    select_n x3, other arithmetic, ppm_sweep(): jnp.where(back_jump * fore_jump > 0, jnp.sign(centred) * magnitude, 0.0)  24.5 us
    concatenate x2, local copies, waits for them, and re-layouts, wrap_pad(): jnp.concatenate([lax.slice_in_dim(values, extent - 3, extent, axis=sweep_...  22.6 us
    reduce_sum x6, other arithmetic, euler_flux(): jnp.sum(velocity * velocity, axis=0)  19.1 us
    sub x3, other arithmetic, ppm_sweep(): 0.5 * (left_flux + right_flux)  18.2 us
  transfers between devices with their start and end apart: 2, of which 1 were waited for; matrix products, arithmetic and copies ran while one was open for 0% of the time, Pallas kernels for 0%

commit v1 on v0

v1 whole, which is shorter than its diff:
```python
import jax
import jax.numpy as jnp
from jax import lax
from jax.experimental import pallas as pl
from jax.experimental.pallas import tpu as pltpu
from jax.sharding import Mesh
from jax.sharding import PartitionSpec as P

WIDE_NARROW = ("wide_0", "wide_1", "wide_2", "narrow_0", "narrow_1")

gamma_minus = 0.4
root_gamma = 1.4**0.5
courant_number = 0.6
smallest = 1e-30

FIELDS = 5
HALO = 3
SEGMENT = 16


def sound_speed(density, pressure):
    return root_gamma * (pressure * lax.rsqrt(jnp.maximum(pressure * density, smallest)))


def primitives(cons):
    density, mom_x, mom_y, mom_z, energy = cons
    inverse = 1.0 / density
    vel_x, vel_y, vel_z = mom_x * inverse, mom_y * inverse, mom_z * inverse
    kinetic = mom_x * vel_x + mom_y * vel_y + mom_z * vel_z
    pressure = gamma_minus * energy - (0.5 * gamma_minus) * kinetic
    return [density, vel_x, vel_y, vel_z, pressure]


def next_segment(value):
    moved = pltpu.roll(value, 7, 0)
    sub = lax.broadcasted_iota(jnp.int32, value.shape, 0)
    return jnp.where(sub == 7, pltpu.roll(moved, 124, 1), moved)


def last_segment(value):
    moved = pltpu.roll(value, 1, 0)
    sub = lax.broadcasted_iota(jnp.int32, value.shape, 0)
    return jnp.where(sub == 0, pltpu.roll(moved, 4, 1), moved)


def jump_of(here, there):
    jump = there - here
    return jnp.abs(jump), jnp.where(jump > 0, 0.5, -0.5)


def slope_of(back, fore):
    sign = back[1] + fore[1]
    size = jnp.minimum(back[0] + fore[0], 4.0 * jnp.minimum(back[0], fore[0]))
    return size * jnp.abs(sign), sign


def edges_of(jump, here, there):
    turn = there[0] - here[0]
    base = 6.0 * jump[0]
    return base - turn, base + turn


def limit(right, left, sign):
    return jnp.minimum(right, 2.0 * left) * sign, jnp.minimum(left, 2.0 * right) * sign


def reconstruct(line, store, count, wrap):
    if wrap:
        jumps = {}
        jumps[count - 1] = jump_of(line(count - 1), next_segment(line(0)))
        jumps[-1] = (last_segment(jumps[count - 1][0]), last_segment(jumps[count - 1][1]))
        slopes = {}
        edges = {}
        for k in range(count):
            if k < count - 1:
                jumps[k] = jump_of(line(k), line(k + 1))
            slopes[k] = slope_of(jumps[k - 1], jumps[k])
            if k >= 1:
                edges[k - 1] = edges_of(jumps[k - 1], slopes[k - 1], slopes[k])
            if k >= 2:
                store(k - 1, limit(edges[k - 1][0], edges[k - 2][1], slopes[k - 1][1]))
        slope_next = (next_segment(slopes[0][0]),)
        edges[count - 1] = edges_of(jumps[count - 1], slopes[count - 1], slope_next)
        store(count - 1, limit(edges[count - 1][0], edges[count - 2][1], slopes[count - 1][1]))
        store(0, limit(edges[0][0], last_segment(edges[count - 1][1]), slopes[0][1]))
        return
    jumps = {-3: jump_of(line(-3), line(-2))}
    slopes, edges = {}, {}
    for k in range(-2, count + 2):
        jumps[k] = jump_of(line(k), line(k + 1))
        slopes[k] = slope_of(jumps[k - 1], jumps[k])
        if k >= -1:
            edges[k - 1] = edges_of(jumps[k - 1], slopes[k - 1], slopes[k])
        if k >= 0:
            store(k - 1, limit(edges[k - 1][0], edges[k - 2][1], slopes[k - 1][1]))


def rusanov(before, behind, normal):
    vn_l, vn_r = before[normal], behind[normal]
    speed = jnp.maximum(
        jnp.abs(vn_l) + sound_speed(before[0], before[4]),
        jnp.abs(vn_r) + sound_speed(behind[0], behind[4]),
    )
    rate_l, rate_r = vn_l + speed, vn_r - speed
    mass_l, mass_r = before[0] * rate_l, behind[0] * rate_r
    mom_l = [before[i] * mass_l for i in (1, 2, 3)]
    mom_r = [behind[i] * mass_r for i in (1, 2, 3)]
    kinetic = (
        (before[1] * mom_l[0] + before[2] * mom_l[1])
        + (before[3] * mom_l[2] + behind[1] * mom_r[0])
        + (behind[2] * mom_r[1] + behind[3] * mom_r[2])
    )
    flux = [mass_l + mass_r] + [mom_l[i] + mom_r[i] for i in range(3)]
    flux[normal] = flux[normal] + (before[4] + behind[4])
    flux.append(
        0.5 * kinetic
        + (before[4] * (2.5 * rate_l + vn_l) + behind[4] * (2.5 * rate_r + vn_r))
    )
    return flux


def march(prim, edge, courant, cons, put, count, normal, half_step, wrap):
    def faces(k):
        sigma, scale = courant(k)
        right, left = [], []
        for f in range(FIELDS):
            value = prim(f, k)
            dist_r, dist_l = edge(f, k)
            mixed = sigma * (dist_r - dist_l)
            right.append(value + scale * (dist_r - mixed))
            left.append(value - scale * (dist_l + mixed))
        return right, left

    def update(k, low, high):
        old = cons(k)
        put(k, [old[f] - half_step * (high[f] - low[f]) for f in range(FIELDS)])

    if wrap:
        right, first_left = faces(0)
        fluxes = {}
        for k in range(count):
            if k < count - 1:
                right_next, left = faces(k + 1)
            else:
                left = [next_segment(v) for v in first_left]
            fluxes[k] = rusanov(right, left, normal)
            if k >= 1:
                update(k, fluxes[k - 1], fluxes[k])
            right = right_next
        update(0, [last_segment(v) for v in fluxes[count - 1]], fluxes[0])
        return
    right, _ = faces(-1)
    low = None
    for k in range(0, count + 1):
        right_next, left = faces(k)
        high = rusanov(right, left, normal)
        if low is not None:
            update(k - 1, low, high)
        low, right = high, right_next


def sweep_line(cons, put, prim_ref, edge_ref, courant_ref, count, normal, step, wrap):
    pad = 0 if wrap else HALO
    for k in range(-pad, count + pad):
        prim = primitives(cons(k))
        for f in range(FIELDS):
            prim_ref[f, k + pad] = prim[f]
        if wrap or -1 <= k <= count:
            sigma = step * (jnp.abs(prim[normal]) + sound_speed(prim[0], prim[4]))
            courant_ref[0, k + pad] = sigma
            courant_ref[1, k + pad] = (1.0 - sigma) * (1.0 / 12.0)

    for f in range(FIELDS):

        def store(k, pair, f=f):
            edge_ref[0, f, k + pad], edge_ref[1, f, k + pad] = pair

        reconstruct(lambda k, f=f: prim_ref[f, k + pad], store, count, wrap)

    march(
        lambda f, k: prim_ref[f, k + pad],
        lambda f, k: (edge_ref[0, f, k + pad], edge_ref[1, f, k + pad]),
        lambda k: (courant_ref[0, k + pad], courant_ref[1, k + pad]),
        cons,
        put,
        count,
        normal,
        0.5 * step,
        wrap,
    )


def peak_kernel(state_ref, peak_ref):
    def body(i, best):
        for half in range(4):
            rows = pl.ds(pl.multiple_of(i * 32 + half * 8, 8), 8)
            prim = primitives([state_ref[f, 0, rows, :] for f in range(FIELDS)])
            sound = sound_speed(prim[0], prim[4])
            best = jnp.maximum(best, jnp.maximum(jnp.abs(prim[1]), jnp.abs(prim[2])) + sound)
        return best

    best = lax.fori_loop(0, 4, body, jnp.zeros((8, 128), jnp.float32))

    @pl.when(pl.program_id(0) == 0)
    def _():
        peak_ref[...] = best

    @pl.when(pl.program_id(0) > 0)
    def _():
        peak_ref[...] = jnp.maximum(peak_ref[...], best)


def peak_call(view):
    rows = view.shape[1]
    return pl.pallas_call(
        peak_kernel,
        grid=(rows,),
        in_specs=[pl.BlockSpec((FIELDS, 1, 128, 128), lambda i: (0, i, 0, 0))],
        out_specs=pl.BlockSpec((8, 128), lambda i: (0, 0)),
        out_shape=jax.ShapeDtypeStruct((8, 128), jnp.float32),
        name="peak",
    )(view)


def window_kernel(
    state_ref, low_ref, high_ref, peaks_ref, out_ref, swept, done, turned, back, prim, edge, courant
):
    rows = state_ref.shape[1]
    peak = jnp.max(peaks_ref[...])
    step = courant_number / jnp.full((8, 128), peak, jnp.float32)
    half = 0.5 * step

    def first_sweep(source, source_row, row):
        for f in range(FIELDS):
            turned[f] = source[f, source_row].T

        def cons(k):
            return [turned[f, pl.ds(k, 8, stride=SEGMENT), :] for f in range(FIELDS)]

        def put(k, new):
            for f in range(FIELDS):
                swept[f, row, k] = new[f]

        sweep_line(cons, put, prim, edge, courant, SEGMENT, 1, half, True)

    def low_body(i, carry):
        first_sweep(low_ref, i, i)
        return carry

    def high_body(i, carry):
        first_sweep(high_ref, i, i + HALO + rows)
        return carry

    def state_body(i, carry):
        first_sweep(state_ref, i, i + HALO)
        return carry

    lax.fori_loop(0, HALO, low_body, 0)
    lax.fori_loop(0, rows, state_body, 0)
    lax.fori_loop(0, HALO, high_body, 0)

    def column(t, carry):
        def cons(k):
            return [swept[f, k + HALO, t] for f in range(FIELDS)]

        def put(k, new):
            for f in range(FIELDS):
                done[f, k, t] = new[f]

        sweep_line(cons, put, prim, edge, courant, rows, 2, step, False)
        return carry

    lax.fori_loop(0, SEGMENT, column, 0)

    def last_sweep(i, carry):
        def cons(k):
            return [done[f, i, k] for f in range(FIELDS)]

        def put(k, new):
            for f in range(FIELDS):
                back[f, pl.ds(k, 8, stride=SEGMENT), :] = new[f]

        sweep_line(cons, put, prim, edge, courant, SEGMENT, 1, half, True)
        for f in range(FIELDS):
            out_ref[f, i] = back[f].T
        return carry

    lax.fori_loop(0, rows, last_sweep, 0)


def window_call(view, low, high, peaks):
    rows = view.shape[1]
    padded = rows + 2 * HALO
    return pl.pallas_call(
        window_kernel,
        in_specs=[pl.BlockSpec(memory_space=pltpu.VMEM)] * 4,
        out_specs=pl.BlockSpec(memory_space=pltpu.VMEM),
        out_shape=jax.ShapeDtypeStruct(view.shape, jnp.float32),
        scratch_shapes=[
            pltpu.VMEM((FIELDS, padded, SEGMENT, 8, 128), jnp.float32),
            pltpu.VMEM((FIELDS, rows, SEGMENT, 8, 128), jnp.float32),
            pltpu.VMEM((FIELDS, 128, 128), jnp.float32),
            pltpu.VMEM((FIELDS, 128, 128), jnp.float32),
            pltpu.VMEM((FIELDS, padded, 8, 128), jnp.float32),
            pltpu.VMEM((2, FIELDS, padded, 8, 128), jnp.float32),
            pltpu.VMEM((2, padded, 8, 128), jnp.float32),
        ],
        compiler_params=pltpu.CompilerParams(vmem_limit_bytes=56 * 1024 * 1024),
        name="window",
    )(view, low, high, peaks)


def local(state):
    fields, rows, planes, columns = state.shape
    tiles = columns // 128
    view = state.reshape(fields, rows, planes, tiles, 128).transpose(0, 1, 3, 2, 4)
    view = view.reshape(fields, rows, tiles * planes, 128)
    devices = 1
    for axis in WIDE_NARROW:
        devices *= lax.axis_size(axis)
    up = [(i, (i + 1) % devices) for i in range(devices)]
    low = lax.ppermute(view[:, rows - HALO :], WIDE_NARROW, up)
    high = lax.ppermute(view[:, :HALO], WIDE_NARROW, [(b, a) for a, b in up])
    peak = jnp.max(peak_call(view), axis=0, keepdims=True)
    peaks = lax.all_to_all(
        jnp.broadcast_to(peak, (devices, 128)), WIDE_NARROW, 0, 0, tiled=True
    )
    out = window_call(view, low, high, peaks)
    out = out.reshape(fields, rows, tiles, planes, 128).transpose(0, 1, 3, 2, 4)
    return out.reshape(fields, rows, planes, columns)


def solution(mesh):
    split = Mesh(
        mesh.devices.reshape(4, 2, 2, 2, 4), ("wide_0", "wide_1", "wide_2", "narrow_0", "narrow_1")
    )
    placed = (P(None, WIDE_NARROW, None, None),)
    return jax.shard_map(
        local,
        mesh=split,
        in_specs=placed,
        out_specs=P(None, WIDE_NARROW, None, None),
        check_vma=False,
    )
```

time: 390 us -> 86.5 us (0.22); the launches traced: 385 us -> 85.4 us
  other arithmetic: 283 us -> 0.69 us
  Pallas kernels: 0 us -> 53.4 us
  local copies, waits for them, and re-layouts: 35.2 us -> 3.97 us
  blocking collectives: 39.7 us -> 19.1 us
  waiting for transfers between devices: 17.8 us -> 0.01 us
    sub x15 -> x0, other arithmetic: 138 us -> none  [the longest x3 39.5 us: ppm_sweep(): to_right = right_edge - 0.5 * courant * (edge_gap - shrink * curvature)]
    pallas_call x0 -> x2, Pallas kernels: none -> 53.4 us  [the longest x1 43.7 us: window_call(): pl.pallas_call(window_kernel, in_specs=[pl.BlockSpec(memory_space=pltpu.V...]
    pmax x5 -> x0, blocking collectives: 39.7 us -> none  [one_axis_at_a_time(): array = lax.pmax(array, axis)]
    mul x18 -> x0, other arithmetic: 36.4 us -> none  [the longest x3 11.7 us: ppm_sweep(): 0.5 * jnp.maximum(left_speed, right_speed)[None] * (right_cons - left_cons)]
    reduce_sum x10 -> x0, other arithmetic: 33.4 us -> none  [the longest x6 19.1 us: euler_flux(): jnp.sum(velocity * velocity, axis=0)]
    select_n x3 -> x0, other arithmetic: 24.5 us -> none  [ppm_sweep(): jnp.where(back_jump * fore_jump > 0, jnp.sign(centred) * magnitude, 0.0)]
    concatenate x2 -> x0, local copies, waits for them, and re-layouts: 22.6 us -> none  [wrap_pad(): jnp.concatenate([lax.slice_in_dim(values, extent - 3, extent, axis=sweep_...]
    all_to_all x0 -> x1, blocking collectives: none -> 19.1 us  [local(): lax.all_to_all(jnp.broadcast_to(peak, (devices, 128)), WIDE_NARROW, 0, 0,...]
  transfers between devices with their start and end apart: 2 -> 2, of which waited for: 1 -> 0; matrix products, arithmetic and copies ran while one was open for 0% -> 1% of each run, Pallas kernels for 0% -> 11%
where the time goes in v1:
time: 86.5 us; the launch traced here: 85.4 us
  Pallas kernels  53.4 us (62%)
  blocking collectives  19.1 us (22%)
  starting transfers between devices  8.21 us (9%)
  local copies, waits for them, and re-layouts  3.97 us (5%)
    pallas_call x1, Pallas kernels, window_call(): pl.pallas_call(window_kernel, in_specs=[pl.BlockSpec(memory_space=pltpu.V...  43.7 us
    all_to_all x1, blocking collectives, local(): lax.all_to_all(jnp.broadcast_to(peak, (devices, 128)), WIDE_NARROW, 0, 0,...  19.1 us
    pallas_call x1, Pallas kernels, peak_call(): pl.pallas_call(peak_kernel, grid=(rows,), in_specs=[pl.BlockSpec((FIELDS,...  9.73 us
    ppermute x1, starting transfers between devices, local(): high = lax.ppermute(view[:, :HALO], WIDE_NARROW, [(b, a) for a, b in up])  8.21 us
    slice x1, local copies, waits for them, and re-layouts, local(): high = lax.ppermute(view[:, :HALO], WIDE_NARROW, [(b, a) for a, b in up])  2.64 us
  transfers between devices with their start and end apart: 2, of which 0 were waited for; matrix products, arithmetic and copies ran while one was open for 1% of the time, Pallas kernels for 11%

profile of v1, /device:TPU:0, one launch (start us, length us, event | category | flops | bytes accessed | tf_op | source)
XLA Modules:
  0.0 85.4 jit_solution(11794651462367213918)
XLA Ops:
  0.0 2.6 %fusion = (f32[5,3,128,128]{3,2,1,0:T(8,128)}, f32[5,3,128,128]{3,2,1,0:T(8,128)S(1)}) fusion(f32[5,16,128,128]{3,2,1,0:T(8,128)} %bitcast.11), kind=kLoop, calls=%fused_computation | loop fusion | bytes 3932160 | tf_op jit(solution)/shard_map/slice | solution.py:323
  2.6 8.2 %collective-permute-start.1 = (f32[5,3,128,128]{3,2,1,0:T(8,128)}, f32[5,3,128,128]{3,2,1,0:T(8,128)S(1)}, u32[]{:S(2)}, u32[]{:S(2)}) collective-permute-start(f32[5,3,128,128]{3,2,1,0:T(8,128)} %get-tuple-element.5), channel_id=1, source_target_pairs={{1,0},{2,1},{3,2},{4,3},{5,4},{6,5},{7,6},{8,7},{9,8},{10,9},{11,1... | collective-permute-start | bytes 2949128 | tf_op jit(solution)/shard_map/ppermute | solution.py:323
  10.9 0.0 collective-permute-start
  10.9 9.7 %peak.1 = f32[8,128]{1,0:T(8,128)} custom-call(f32[5,16,128,128]{3,2,1,0:T(8,128)} %bitcast.12), custom_call_target="tpu_custom_call" | custom-call | tf_op jit(solution)/shard_map/peak/pallas_call | solution.py:215
  20.6 0.7 reduce_max.9
  21.3 19.1 %all_to_all.8 = f32[128,1,128]{2,1,0:T(1,128)} all-to-all(f32[128,1,128]{2,1,0:T(1,128)S(1)} %broadcast_in_dim.2), channel_id=1, replica_groups=mesh['wide_0'=4,'wide_1'=2,'wide_2'=2,'narrow_0'=2,'narrow_1'=4] {'wide_..., dimensions={0} | all-to-all | bytes 131072 | tf_op jit(solution)/shard_map/all_to_all | solution.py:325
  40.4 0.0 collective-permute-done.1.high_ref
  40.4 0.0 copy-start
  40.4 0.0 collective-permute-done.low_ref
  40.4 0.0 copy-start.1
  40.4 1.0 %copy-done = f32[5,3,128,128]{3,2,1,0:T(8,128)} copy-done((f32[5,3,128,128]{3,2,1,0:T(8,128)}, f32[5,3,128,128]{3,2,1,0:T(8,128)S(1)}, u32[]{:S(2)}) %copy-start) | copy-done | bytes 983064
  41.4 0.3 copy-done.1
  41.7 43.7 %window.1 = f32[5,16,128,128]{3,2,1,0:T(8,128)} custom-call(f32[5,16,128,128]{3,2,1,0:T(8,128)} %bitcast.13, f32[5,3,128,128]{3,2,1,0:T(8,128)} %copy-done.1, f32[5,3,128,128]{3,2,1,0:T(8,128)} %copy-done, f32[128,128]{1,0:T(8,128)} %bitcast.14), custom_call_target="tpu_custom_call" | custom-call | tf_op jit(solution)/shard_map/window/pallas_call | solution.py:294
  (1 shorter events, 0.0 us)
Async XLA Ops:
  2.6 37.8 %collective-permute-start.1 = (f32[5,3,128,128]{3,2,1,0:T(8,128)}, f32[5,3,128,128]{3,2,1,0:T(8,128)S(1)}, u32[]{:S(2)}, u32[]{:S(2)}) collective-permute-start(f32[5,3,128,128]{3,2,1,0:T(8,128)} %get-tuple-element.5), channel_id=1, source_target_pairs={{1,0},{2,1},{3,2},{4,3},{5,4},{6,5},{7,6},{8,7},{9,8},{10,9},{11,1... | collective-permute-start | bytes 2949128 | tf_op jit(solution)/shard_map/ppermute | solution.py:323
  10.9 29.6 %collective-permute-start = (f32[5,3,128,128]{3,2,1,0:T(8,128)S(1)}, f32[5,3,128,128]{3,2,1,0:T(8,128)S(1)}, u32[]{:S(2)}, u32[]{:S(2)}) collective-permute-start(f32[5,3,128,128]{3,2,1,0:T(8,128)S(1)} %get-tuple-element.6), channel_id=1, source_target_pairs={{0,1},{1,2},{2,3},{3,4},{4,5},{5,6},{6,7},{7,8},{8,9},{9,10},{10,1... | collective-permute-start | bytes 2949128 | tf_op jit(solution)/shard_map/ppermute | solution.py:322
  40.4 1.0 %copy-start = (f32[5,3,128,128]{3,2,1,0:T(8,128)}, f32[5,3,128,128]{3,2,1,0:T(8,128)S(1)}, u32[]{:S(2)}) copy-start(f32[5,3,128,128]{3,2,1,0:T(8,128)S(1)} %collective-permute-done.1.high_ref) | copy-start | bytes 2949124
  40.4 1.3 %copy-start.1 = (f32[5,3,128,128]{3,2,1,0:T(8,128)}, f32[5,3,128,128]{3,2,1,0:T(8,128)S(1)}, u32[]{:S(2)}) copy-start(f32[5,3,128,128]{3,2,1,0:T(8,128)S(1)} %collective-permute-done.low_ref) | copy-start | bytes 2949124

commit v2 on v1

v2 whole, which is shorter than its diff:
```python
import jax
import jax.numpy as jnp
from jax import lax
from jax.experimental import pallas as pl
from jax.experimental.pallas import tpu as pltpu
from jax.sharding import Mesh
from jax.sharding import PartitionSpec as P

WIDE_NARROW = ("wide_0", "wide_1", "wide_2", "narrow_0", "narrow_1")

gamma_minus = 0.4
root_gamma = 1.4**0.5
courant_number = 0.6
smallest = 1e-30

FIELDS = 5
HALO = 3
SEGMENT = 16


def sound_speed(density, pressure, scale=1.0):
    return (root_gamma * scale) * (
        pressure * lax.rsqrt(jnp.maximum(pressure * density, smallest))
    )


def primitives(cons):
    density, mom_x, mom_y, mom_z, energy = cons
    inverse = 1.0 / density
    vel_x, vel_y, vel_z = mom_x * inverse, mom_y * inverse, mom_z * inverse
    kinetic = mom_x * vel_x + mom_y * vel_y + mom_z * vel_z
    pressure = gamma_minus * energy - (0.5 * gamma_minus) * kinetic
    return [density, vel_x, vel_y, vel_z, pressure]


def next_segment(value):
    moved = pltpu.roll(value, 7, 0)
    sub = lax.broadcasted_iota(jnp.int32, value.shape, 0)
    return jnp.where(sub == 7, pltpu.roll(moved, 124, 1), moved)


def last_segment(value):
    moved = pltpu.roll(value, 1, 0)
    sub = lax.broadcasted_iota(jnp.int32, value.shape, 0)
    return jnp.where(sub == 0, pltpu.roll(moved, 4, 1), moved)


class Lazy(dict):
    def __init__(self, make):
        super().__init__()
        self.make = make

    def __missing__(self, k):
        value = self[k] = self.make(k)
        return value


def make_reconstruct(cell, courant):
    def jump(k):
        step = cells[k + 1] - cells[k]
        return jnp.abs(step), step > 0

    def slope(k):
        (back, back_up), (fore, fore_up) = jumps[k - 1], jumps[k]
        turns = jnp.logical_xor(back_up, fore_up)
        size = jnp.minimum(back + fore, 4.0 * jnp.minimum(back, fore))
        return jnp.where(turns, 0.0, size), turns

    def edge(k):
        turn = slopes[k + 1][0] - slopes[k][0]
        base = 6.0 * jumps[k][0]
        return base - turn, base + turn

    def faces(k):
        right, left = edges[k][0], edges[k - 1][1]
        right, left = jnp.minimum(right, 2.0 * left), jnp.minimum(left, 2.0 * right)
        sigma, scale = courant(k)
        signed = jnp.where(slopes[k][1], 0.0, jnp.where(jumps[k][1], scale, -scale))
        mixed = sigma * (right - left)
        return cells[k] + signed * (right - mixed), cells[k] - signed * (left + mixed)

    cells, jumps, slopes, edges = Lazy(cell), Lazy(jump), Lazy(slope), Lazy(edge)
    return faces


def rusanov(before, behind, normal, step):
    half = 0.5 * step
    vn_l, vn_r = half * before[normal], half * behind[normal]
    speed = jnp.maximum(
        jnp.abs(vn_l) + sound_speed(before[0], before[4], half),
        jnp.abs(vn_r) + sound_speed(behind[0], behind[4], half),
    )
    rate_l, rate_r = vn_l + speed, vn_r - speed
    mass_l, mass_r = before[0] * rate_l, behind[0] * rate_r
    mom_l = [before[i] * mass_l for i in (1, 2, 3)]
    mom_r = [behind[i] * mass_r for i in (1, 2, 3)]
    kinetic = (
        (before[1] * mom_l[0] + before[2] * mom_l[1])
        + (before[3] * mom_l[2] + behind[1] * mom_r[0])
        + (behind[2] * mom_r[1] + behind[3] * mom_r[2])
    )
    flux = [mass_l + mass_r] + [mom_l[i] + mom_r[i] for i in range(3)]
    flux[normal] = flux[normal] + half * (before[4] + behind[4])
    flux.append(
        0.5 * kinetic
        + (before[4] * (2.5 * rate_l + vn_l) + behind[4] * (2.5 * rate_r + vn_r))
    )
    return flux


def sweep_line(cons, put, scratch, count, normal, step, wrap, beside=None):
    prim_ref, face_ref, courant_ref = scratch
    first = 0 if wrap else -HALO
    last = count if wrap else count + HALO
    reach = HALO

    def start(k):
        prim = primitives(cons(k))
        for f in range(FIELDS):
            prim_ref[f, k + reach] = prim[f]
        if wrap or -1 <= k <= count:
            sigma = step * jnp.abs(prim[normal]) + sound_speed(prim[0], prim[4], step)
            courant_ref[0, k + reach] = sigma
            courant_ref[1, k + reach] = (1.0 / 12.0) - (1.0 / 12.0) * sigma
        return prim

    if wrap:
        for k in (0, 1):
            prim = start(k)
            for f in range(FIELDS):
                prim_ref[f, count + k + reach] = next_segment(prim[f])
        for k in (count - 2, count - 1):
            prim = start(k)
            for f in range(FIELDS):
                prim_ref[f, k - count + reach] = last_segment(prim[f])
        for k in range(2, count - 2):
            start(k)
        order = [*range(2, count), 0, 1]
    else:
        for k in range(first, last):
            start(k)
        order = list(range(-1, count + 1))

    for f in range(FIELDS):
        if beside is not None:
            beside(f)
        faces = make_reconstruct(
            lambda k, f=f: prim_ref[f, k + reach],
            lambda k: (courant_ref[0, k + reach], courant_ref[1, k + reach]),
        )
        for k in order:
            face_ref[0, f, k + reach], face_ref[1, f, k + reach] = faces(k)

    def flux(k, behind=None):
        before = [face_ref[0, f, k + reach] for f in range(FIELDS)]
        if behind is None:
            behind = [face_ref[1, f, k + 1 + reach] for f in range(FIELDS)]
        return rusanov(before, behind, normal, step)

    def update(k, low, high):
        old = cons(k)
        put(k, [old[f] + (low[f] - high[f]) for f in range(FIELDS)])

    if wrap:
        behind = [next_segment(face_ref[1, f, reach]) for f in range(FIELDS)]
        front = low = flux(0)
        middle = count // 2
        for k in range(1, count):
            if k == middle:
                end = flux(count - 1, behind)
                into = [last_segment(v) for v in end]
            high = flux(k) if k < count - 1 else end
            update(k, low, high)
            low = high
        update(0, into, front)
        return
    low = flux(-1)
    for k in range(count):
        high = flux(k)
        update(k, low, high)
        low = high


PEAK_STEPS = 4


def peak_kernel(state_ref, peak_ref, best_ref):
    rows = state_ref.shape[1]
    place = pl.program_id(0)

    def body(i, best):
        best = list(best)
        for row in range(rows):
            at = pl.ds(pl.multiple_of(i * 8, 8), 8)
            prim = primitives([state_ref[f, row, at, :] for f in range(FIELDS)])
            sound = sound_speed(prim[0], prim[4])
            new = jnp.maximum(jnp.abs(prim[1]), jnp.abs(prim[2])) + sound
            best[row] = jnp.maximum(best[row], new)
        return tuple(best)

    zero = jnp.zeros((8, 128), jnp.float32)
    parts = lax.fori_loop(0, 16, body, (zero,) * rows, unroll=4)
    best = parts[0]
    for part in parts[1:]:
        best = jnp.maximum(best, part)

    @pl.when(place == 0)
    def _():
        best_ref[...] = best

    @pl.when(place > 0)
    def _():
        best_ref[...] = jnp.maximum(best_ref[...], best)

    @pl.when(place == PEAK_STEPS - 1)
    def _():
        peak_ref[...] = jnp.full(peak_ref.shape, jnp.max(best_ref[...]), jnp.float32)


def peak_call(view, devices):
    rows = view.shape[1]
    return pl.pallas_call(
        peak_kernel,
        grid=(PEAK_STEPS,),
        in_specs=[pl.BlockSpec((FIELDS, rows // PEAK_STEPS, 128, 128), lambda i: (0, i, 0, 0))],
        out_specs=pl.BlockSpec((devices, 128), lambda i: (0, 0)),
        out_shape=jax.ShapeDtypeStruct((devices, 128), jnp.float32),
        scratch_shapes=[pltpu.VMEM((8, 128), jnp.float32)],
        name="peak",
    )(view)


def border_kernel(high_ref, low_ref, peak_ref, up_ref, down_ref):
    up_ref[...] = high_ref[...]
    down_ref[...] = low_ref[...]


def border_call(view, peak):
    rows = view.shape[1]
    edge = jax.ShapeDtypeStruct((FIELDS, HALO, 128, 128), jnp.float32)
    block = (FIELDS, 1, 128, 128)
    return pl.pallas_call(
        border_kernel,
        grid=(HALO,),
        in_specs=[
            pl.BlockSpec(block, lambda i: (0, i + rows - HALO, 0, 0)),
            pl.BlockSpec(block, lambda i: (0, i, 0, 0)),
            pl.BlockSpec(memory_space=pl.ANY),
        ],
        out_specs=[pl.BlockSpec(block, lambda i: (0, i, 0, 0))] * 2,
        out_shape=[edge, edge],
        name="border",
    )(view, view, peak)


def turn(turned, slot, f, tile):
    flat = tile.T
    for v in range(128 // 8):
        place = (v % 2) * 64 + v // 2
        turned[slot, f, pl.ds(place, 8, stride=8), :] = flat[v * 8 : (v + 1) * 8]


def first_sweep(turned, slot, swept, row, scratch, half, beside):
    def cons(k):
        return [turned[slot, f, k * 8 : (k + 1) * 8, :] for f in range(FIELDS)]

    def put(k, new):
        for f in range(FIELDS):
            swept[f, row, k] = new[f]

    sweep_line(cons, put, scratch, SEGMENT, 1, half, True, beside)


def turn_back(final, row, back, slot, f):
    final[f, row] = back[slot, f].T


def last_sweep(done, row, back, slot, scratch, half, beside):
    def cons(k):
        return [done[f, row, k] for f in range(FIELDS)]

    def put(k, new):
        for f in range(FIELDS):
            back[slot, f, pl.ds(k, 8, stride=SEGMENT), :] = new[f]

    sweep_line(cons, put, scratch, SEGMENT, 1, half, True, beside)


def cross_sweep(swept, done, count, row, t, scratch, step):
    def cons(k):
        return [swept[f, k + HALO, t] for f in range(FIELDS)]

    def put(k, new):
        for f in range(FIELDS):
            done[f, k + row, t] = new[f]

    sweep_line(cons, put, scratch, count, 2, step, False)


def finish(done, final, back, scratch, half, count, row_out):
    def two_rows(i, carry):
        row = 2 * i
        earlier = jnp.maximum(row - 1, 0)
        last_sweep(
            done, row, back, 0, scratch, half, lambda f: turn_back(final, earlier, back, 1, f)
        )
        last_sweep(
            done, row + 1, back, 1, scratch, half, lambda f: turn_back(final, row, back, 0, f)
        )

        @pl.when(i > 0)
        def _():
            row_out(earlier).start()

        row_out(row).start()
        return carry

    lax.fori_loop(0, count // 2, two_rows, 0)
    for f in range(FIELDS):
        turn_back(final, count - 1, back, 1, f)
    row_out(count - 1).start()


def time_step(peaks_ref):
    peak = jnp.max(peaks_ref[...])
    step = courant_number / jnp.full((8, 128), peak, jnp.float32)
    return step, 0.5 * step


def inner_kernel(
    state_ref, peaks_ref, out_ref, rim_ref,
    raw, swept, done, final, turned, back, prim, face, courant, in_sems, out_sems, rim_sems,
):
    rows = state_ref.shape[1]
    inner = rows - 2 * HALO
    scratch = (prim, face, courant)

    def row_in(i):
        return pltpu.make_async_copy(state_ref.at[:, i], raw.at[:, i], in_sems.at[i])

    def row_out(i):
        return pltpu.make_async_copy(final.at[:, i], out_ref.at[:, i + HALO], out_sems.at[i])

    for i in range(rows):
        row_in(i).start()
    step, half = time_step(peaks_ref)
    row_in(0).wait()
    for f in range(FIELDS):
        turn(turned, 0, f, raw[f, 0])

    def two_rows(i, carry):
        row = 2 * i
        later = jnp.minimum(row + 2, rows - 1)
        row_in(row + 1).wait()

        @pl.when(row + 2 < rows)
        def _():
            row_in(later).wait()

        first_sweep(
            turned, 0, swept, row, scratch, half,
            lambda f: turn(turned, 1, f, raw[f, row + 1]),
        )
        first_sweep(
            turned, 1, swept, row + 1, scratch, half,
            lambda f: turn(turned, 0, f, raw[f, later]),
        )
        return carry

    lax.fori_loop(0, rows // 2, two_rows, 0)

    rims = (
        pltpu.make_async_copy(
            swept.at[:, pl.ds(0, 2 * HALO)], rim_ref.at[:, pl.ds(0, 2 * HALO)], rim_sems.at[0]
        ),
        pltpu.make_async_copy(
            swept.at[:, pl.ds(rows - 2 * HALO, 2 * HALO)],
            rim_ref.at[:, pl.ds(2 * HALO, 2 * HALO)],
            rim_sems.at[1],
        ),
    )
    for copy in rims:
        copy.start()

    def column(t, carry):
        cross_sweep(swept, done, inner, 0, t, scratch, step)
        return carry

    lax.fori_loop(0, SEGMENT, column, 0)
    finish(done, final, back, scratch, half, inner, row_out)
    for copy in rims:
        copy.wait()
    for i in range(inner):
        row_out(i).wait()


def outer_kernel(
    rim_ref, low_ref, high_ref, peaks_ref, half_done_ref, out_ref,
    raw, lower, upper, done, final, turned, back, prim, face, courant, in_sems, out_sems,
):
    rows = out_ref.shape[1]
    scratch = (prim, face, courant)
    copies = (
        pltpu.make_async_copy(low_ref, raw.at[:, pl.ds(0, HALO)], in_sems.at[0]),
        pltpu.make_async_copy(high_ref, raw.at[:, pl.ds(HALO, HALO)], in_sems.at[1]),
        pltpu.make_async_copy(
            rim_ref.at[:, pl.ds(0, 2 * HALO)], lower.at[:, pl.ds(HALO, 2 * HALO)], in_sems.at[2]
        ),
        pltpu.make_async_copy(
            rim_ref.at[:, pl.ds(2 * HALO, 2 * HALO)], upper.at[:, pl.ds(0, 2 * HALO)], in_sems.at[3]
        ),
    )

    def row_out(i):
        place = jnp.where(i < HALO, i, i + (rows - 2 * HALO))
        return pltpu.make_async_copy(final.at[:, i], out_ref.at[:, place], out_sems.at[i])

    for copy in copies:
        copy.start()
    step, half = time_step(peaks_ref)
    copies[0].wait()
    for f in range(FIELDS):
        turn(turned, 0, f, raw[f, 0])
    copies[1].wait()

    def two_rows(i, carry):
        later = jnp.minimum(i + 1, HALO - 1)
        first_sweep(
            turned, 0, lower, i, scratch, half,
            lambda f: turn(turned, 1, f, raw[f, i + HALO]),
        )
        first_sweep(
            turned, 1, upper, i + 2 * HALO, scratch, half,
            lambda f: turn(turned, 0, f, raw[f, later]),
        )
        return carry

    lax.fori_loop(0, HALO, two_rows, 0)
    copies[2].wait()
    copies[3].wait()

    def column(t, carry):
        cross_sweep(lower, done, HALO, 0, t, scratch, step)
        cross_sweep(upper, done, HALO, HALO, t, scratch, step)
        return carry

    lax.fori_loop(0, SEGMENT, column, 0)
    finish(done, final, back, scratch, half, 2 * HALO, row_out)
    for i in range(2 * HALO):
        row_out(i).wait()


def line_scratch(length):
    return [
        pltpu.VMEM((2, FIELDS, 128, 128), jnp.float32),
        pltpu.VMEM((2, FIELDS, 128, 128), jnp.float32),
        pltpu.VMEM((FIELDS, length + 2 * HALO, 8, 128), jnp.float32),
        pltpu.VMEM((2, FIELDS, length + 2 * HALO, 8, 128), jnp.float32),
        pltpu.VMEM((2, length + 2 * HALO, 8, 128), jnp.float32),
    ]


def inner_call(view, peaks):
    rows = view.shape[1]
    inner = rows - 2 * HALO
    anywhere = pl.BlockSpec(memory_space=pl.ANY)
    return pl.pallas_call(
        inner_kernel,
        in_specs=[anywhere, pl.BlockSpec(memory_space=pltpu.VMEM)],
        out_specs=[anywhere, anywhere],
        out_shape=[
            jax.ShapeDtypeStruct(view.shape, jnp.float32),
            jax.ShapeDtypeStruct((FIELDS, 4 * HALO, SEGMENT, 8, 128), jnp.float32),
        ],
        scratch_shapes=[
            pltpu.VMEM((FIELDS, rows, 128, 128), jnp.float32),
            pltpu.VMEM((FIELDS, rows, SEGMENT, 8, 128), jnp.float32),
            pltpu.VMEM((FIELDS, inner, SEGMENT, 8, 128), jnp.float32),
            pltpu.VMEM((FIELDS, inner, 128, 128), jnp.float32),
            *line_scratch(SEGMENT),
            pltpu.SemaphoreType.DMA((rows,)),
            pltpu.SemaphoreType.DMA((inner,)),
            pltpu.SemaphoreType.DMA((2,)),
        ],
        compiler_params=pltpu.CompilerParams(vmem_limit_bytes=48 * 1024 * 1024),
        name="inner",
    )(view, peaks)


def outer_call(rim, low, high, peaks, half_done):
    anywhere = pl.BlockSpec(memory_space=pl.ANY)
    return pl.pallas_call(
        outer_kernel,
        in_specs=[anywhere, anywhere, anywhere, pl.BlockSpec(memory_space=pltpu.VMEM), anywhere],
        out_specs=anywhere,
        out_shape=jax.ShapeDtypeStruct(half_done.shape, jnp.float32),
        input_output_aliases={4: 0},
        scratch_shapes=[
            pltpu.VMEM((FIELDS, 2 * HALO, 128, 128), jnp.float32),
            pltpu.VMEM((FIELDS, 3 * HALO, SEGMENT, 8, 128), jnp.float32),
            pltpu.VMEM((FIELDS, 3 * HALO, SEGMENT, 8, 128), jnp.float32),
            pltpu.VMEM((FIELDS, 2 * HALO, SEGMENT, 8, 128), jnp.float32),
            pltpu.VMEM((FIELDS, 2 * HALO, 128, 128), jnp.float32),
            *line_scratch(SEGMENT),
            pltpu.SemaphoreType.DMA((4,)),
            pltpu.SemaphoreType.DMA((2 * HALO,)),
        ],
        compiler_params=pltpu.CompilerParams(vmem_limit_bytes=48 * 1024 * 1024),
        name="outer",
    )(rim, low, high, peaks, half_done)


def local(state):
    fields, rows, planes, columns = state.shape
    tiles = columns // 128
    view = state.reshape(fields, rows, planes, tiles, 128).transpose(0, 1, 3, 2, 4)
    view = view.reshape(fields, rows, tiles * planes, 128)
    devices = 1
    for axis in WIDE_NARROW:
        devices *= lax.axis_size(axis)
    up = [(i, (i + 1) % devices) for i in range(devices)]
    peak = peak_call(view, devices)
    peaks = lax.all_to_all(peak, WIDE_NARROW, 0, 0, tiled=True)
    send_up, send_down = border_call(view, peaks)
    low = lax.ppermute(send_up, WIDE_NARROW, up)
    high = lax.ppermute(send_down, WIDE_NARROW, [(b, a) for a, b in up])
    out, rim = inner_call(view, peaks)
    out = outer_call(rim, low, high, peaks, out)
    out = out.reshape(fields, rows, tiles, planes, 128).transpose(0, 1, 3, 2, 4)
    return out.reshape(fields, rows, planes, columns)


def solution(mesh):
    split = Mesh(
        mesh.devices.reshape(4, 2, 2, 2, 4), ("wide_0", "wide_1", "wide_2", "narrow_0", "narrow_1")
    )
    placed = (P(None, WIDE_NARROW, None, None),)
    return jax.shard_map(
        local,
        mesh=split,
        in_specs=placed,
        out_specs=P(None, WIDE_NARROW, None, None),
        check_vma=False,
    )
```

time: 86.5 us -> 75.5 us (0.87)
  Pallas kernels: 53.4 us -> 47.1 us
  local copies, waits for them, and re-layouts: 3.97 us -> 0.01 us
  blocking collectives: 19.1 us -> 20.9 us
  starting transfers between devices: 8.21 us -> 7.18 us
    pallas_call x2 -> x4, Pallas kernels: 53.4 us -> 47.1 us  [the longest x1 24.7 us: inner_call(): pl.pallas_call(inner_kernel, in_specs=[anywhere, pl.BlockSpec(memory_spac...]
    slice x1 -> x0, local copies, waits for them, and re-layouts: 2.64 us -> none  [local(): high = lax.ppermute(view[:, :HALO], WIDE_NARROW, [(b, a) for a, b in up])]
    all_to_all x1, blocking collectives: 19.1 us -> 20.9 us  [local(): peaks = lax.all_to_all(peak, WIDE_NARROW, 0, 0, tiled=True)]
    unnamed x4 -> x2, local copies, waits for them, and re-layouts: 1.29 us -> 0.01 us
    ppermute x2, starting transfers between devices: 8.21 us -> 7.18 us  [the longest x1 6.34 us: local(): high = lax.ppermute(send_down, WIDE_NARROW, [(b, a) for a, b in up])]
  transfers between devices with their start and end apart: 2 -> 2, of which waited for: 0 -> 0; matrix products, arithmetic and copies ran while one was open for 1% -> 0% of each run, Pallas kernels for 11% -> 33%
where the time goes in v2:
time: 75.5 us; the launch traced here: 75.2 us
  Pallas kernels  47.1 us (62%)
  blocking collectives  20.9 us (28%)
  starting transfers between devices  7.18 us (10%)
    pallas_call x1, Pallas kernels, inner_call(): pl.pallas_call(inner_kernel, in_specs=[anywhere, pl.BlockSpec(memory_spac...  24.7 us
    all_to_all x1, blocking collectives, local(): peaks = lax.all_to_all(peak, WIDE_NARROW, 0, 0, tiled=True)  20.9 us
    pallas_call x1, Pallas kernels, outer_call(): pl.pallas_call(outer_kernel, in_specs=[anywhere, anywhere, anywhere, pl.B...  14.4 us
    ppermute x1, starting transfers between devices, local(): high = lax.ppermute(send_down, WIDE_NARROW, [(b, a) for a, b in up])  6.34 us
    pallas_call x1, Pallas kernels, peak_call(): pl.pallas_call(peak_kernel, grid=(PEAK_STEPS,), in_specs=[pl.BlockSpec((F...  4.38 us
    pallas_call x1, Pallas kernels, border_call(): pl.pallas_call(border_kernel, grid=(HALO,), in_specs=[pl.BlockSpec(block,...  3.65 us
  transfers between devices with their start and end apart: 2, of which 0 were waited for; matrix products, arithmetic and copies ran while one was open for 0% of the time, Pallas kernels for 33%

profile of v2, /device:TPU:0, one launch (start us, length us, event | category | flops | bytes accessed | tf_op | source)
XLA Modules:
  0.0 75.2 jit_solution(1741190708724545674)
XLA Ops:
  0.0 4.4 %peak.1 = f32[128,128]{1,0:T(8,128)} custom-call(f32[5,16,128,128]{3,2,1,0:T(8,128)} %bitcast.17), custom_call_target="tpu_custom_call" | custom-call | tf_op jit(solution)/shard_map/peak/pallas_call | solution.py:222
  4.4 20.9 %all_to_all.11 = f32[128,1,128]{2,1,0:T(1,128)} all-to-all(f32[128,1,128]{2,1,0:T(1,128)} %bitcast.21), channel_id=1, replica_groups=mesh['wide_0'=4,'wide_1'=2,'wide_2'=2,'narrow_0'=2,'narrow_1'=4] {'wide_..., dimensions={0} | all-to-all | bytes 131072 | tf_op jit(solution)/shard_map/all_to_all | solution.py:523
  25.3 0.0 copy-start
  25.3 3.7 %border.1 = (f32[5,3,128,128]{3,2,1,0:T(8,128)}, f32[5,3,128,128]{3,2,1,0:T(8,128)}) custom-call(f32[5,16,128,128]{3,2,1,0:T(8,128)} %bitcast.18, f32[5,16,128,128]{3,2,1,0:T(8,128)} %bitcast.19, f32[128,128]{1,0:T(8,128)} %bitcast.14), custom_call_target="tpu_custom_call" | custom-call | tf_op jit(solution)/shard_map/border/pallas_call | solution.py:242
  28.9 0.8 %collective-permute-start = (f32[5,3,128,128]{3,2,1,0:T(8,128)}, f32[5,3,128,128]{3,2,1,0:T(8,128)S(1)}, u32[]{:S(2)}, u32[]{:S(2)}) collective-permute-start(f32[5,3,128,128]{3,2,1,0:T(8,128)} %get-tuple-element.10), channel_id=1, source_target_pairs={{0,1},{1,2},{2,3},{3,4},{4,5},{5,6},{6,7},{7,8},{8,9},{9,10},{10,1... | collective-permute-start | bytes 2949128 | tf_op jit(solution)/shard_map/ppermute | solution.py:525
  29.8 6.3 %collective-permute-start.1 = (f32[5,3,128,128]{3,2,1,0:T(8,128)}, f32[5,3,128,128]{3,2,1,0:T(8,128)S(1)}, u32[]{:S(2)}, u32[]{:S(2)}) collective-permute-start(f32[5,3,128,128]{3,2,1,0:T(8,128)} %get-tuple-element.11), channel_id=1, source_target_pairs={{1,0},{2,1},{3,2},{4,3},{5,4},{6,5},{7,6},{8,7},{9,8},{10,9},{11,1... | collective-permute-start | bytes 2949128 | tf_op jit(solution)/shard_map/ppermute | solution.py:526
  36.1 0.0 copy-done
  36.1 24.7 %inner.1 = (f32[5,16,128,128]{3,2,1,0:T(8,128)}, f32[5,12,16,8,128]{4,3,2,1,0:T(8,128)S(1)}) custom-call(f32[5,16,128,128]{3,2,1,0:T(8,128)} %bitcast.20, f32[128,128]{1,0:T(8,128)S(1)} %bitcast.15), custom_call_target="tpu_custom_call" | custom-call | tf_op jit(solution)/shard_map/inner/pallas_call | solution.py:467
  60.8 0.0 collective-permute-done.low_ref
  60.8 0.0 collective-permute-done.1.high_ref
  60.8 14.4 %outer.1 = f32[5,16,128,128]{3,2,1,0:T(8,128)} custom-call(f32[5,12,16,8,128]{4,3,2,1,0:T(8,128)S(1)} %get-tuple-element.9.rim_ref, f32[5,3,128,128]{3,2,1,0:T(8,128)S(1)} %collective-permute-done.low_ref, f32[5,3,128,128]{3,2,1,0:T(8,128)S(1)} %collective-permute-done.1.high_ref, f32[128,128]{1,0:T(8,128)S(1)} %bitcast.16, ...), custom_call_target="tpu_custom_call", output_to_operand_aliasing={{}: (4, {})} | custom-call | tf_op jit(solution)/shard_map/outer/pallas_call | solution.py:492
Async XLA Ops:
  25.3 10.8 %copy-start = (f32[128,1,128]{2,1,0:T(1,128)S(1)}, f32[128,1,128]{2,1,0:T(1,128)}, u32[]{:S(2)}) copy-start(f32[128,1,128]{2,1,0:T(1,128)} %all_to_all.11) | copy-start | bytes 196612
  28.9 31.9 %collective-permute-start = (f32[5,3,128,128]{3,2,1,0:T(8,128)}, f32[5,3,128,128]{3,2,1,0:T(8,128)S(1)}, u32[]{:S(2)}, u32[]{:S(2)}) collective-permute-start(f32[5,3,128,128]{3,2,1,0:T(8,128)} %get-tuple-element.10), channel_id=1, source_target_pairs={{0,1},{1,2},{2,3},{3,4},{4,5},{5,6},{6,7},{7,8},{8,9},{9,10},{10,1... | collective-permute-start | bytes 2949128 | tf_op jit(solution)/shard_map/ppermute | solution.py:525
  29.8 31.1 %collective-permute-start.1 = (f32[5,3,128,128]{3,2,1,0:T(8,128)}, f32[5,3,128,128]{3,2,1,0:T(8,128)S(1)}, u32[]{:S(2)}, u32[]{:S(2)}) collective-permute-start(f32[5,3,128,128]{3,2,1,0:T(8,128)} %get-tuple-element.11), channel_id=1, source_target_pairs={{1,0},{2,1},{3,2},{4,3},{5,4},{6,5},{7,6},{8,7},{9,8},{10,9},{11,1... | collective-permute-start | bytes 2949128 | tf_op jit(solution)/shard_map/ppermute | solution.py:526

commit v3 on v2

--- a/solution.py
+++ b/solution.py
@@ -76,8 +76,9 @@
         right, left = jnp.minimum(right, 2.0 * left), jnp.minimum(left, 2.0 * right)
         sigma, scale = courant(k)
         signed = jnp.where(slopes[k][1], 0.0, jnp.where(jumps[k][1], scale, -scale))
-        mixed = sigma * (right - left)
-        return cells[k] + signed * (right - mixed), cells[k] - signed * (left + mixed)
+        right, left = signed * right, signed * left
+        base = cells[k] - sigma * (right - left)
+        return base + right, base - left
 
     cells, jumps, slopes, edges = Lazy(cell), Lazy(jump), Lazy(slope), Lazy(edge)
     return faces
@@ -108,77 +109,90 @@
     return flux
 
 
-def sweep_line(cons, put, scratch, count, normal, step, wrap, beside=None):
-    prim_ref, face_ref, courant_ref = scratch
-    first = 0 if wrap else -HALO
-    last = count if wrap else count + HALO
-    reach = HALO
-
-    def start(k):
-        prim = primitives(cons(k))
-        for f in range(FIELDS):
-            prim_ref[f, k + reach] = prim[f]
-        if wrap or -1 <= k <= count:
-            sigma = step * jnp.abs(prim[normal]) + sound_speed(prim[0], prim[4], step)
-            courant_ref[0, k + reach] = sigma
-            courant_ref[1, k + reach] = (1.0 / 12.0) - (1.0 / 12.0) * sigma
-        return prim
-
-    if wrap:
+class Line:
+    def __init__(self, cons, put, scratch, count, normal, step, wrap):
+        self.cons, self.put, self.count, self.wrap = cons, put, count, wrap
+        self.prim, self.face, self.courant = scratch
+        self.normal, self.step = normal, step
+
+    def ready(self):
+        count = self.count
+
+        def start(k):
+            prim = primitives(self.cons(k))
+            for f in range(FIELDS):
+                self.prim[f, k + HALO] = prim[f]
+            if self.wrap or -1 <= k <= count:
+                sigma = self.step * jnp.abs(prim[self.normal]) + sound_speed(
+                    prim[0], prim[4], self.step
+                )
+                self.courant[0, k + HALO] = sigma
+                self.courant[1, k + HALO] = (1.0 / 12.0) - (1.0 / 12.0) * sigma
+            return prim
+
+        if not self.wrap:
+            for k in range(-HALO, count + HALO):
+                start(k)
+            return
         for k in (0, 1):
             prim = start(k)
             for f in range(FIELDS):
-                prim_ref[f, count + k + reach] = next_segment(prim[f])
+                self.prim[f, count + k + HALO] = next_segment(prim[f])
         for k in (count - 2, count - 1):
             prim = start(k)
             for f in range(FIELDS):
-                prim_ref[f, k - count + reach] = last_segment(prim[f])
+                self.prim[f, k - count + HALO] = last_segment(prim[f])
         for k in range(2, count - 2):
             start(k)
-        order = [*range(2, count), 0, 1]
-    else:
-        for k in range(first, last):
-            start(k)
-        order = list(range(-1, count + 1))
-
-    for f in range(FIELDS):
-        if beside is not None:
-            beside(f)
+
+    def rebuild(self, f):
         faces = make_reconstruct(
-            lambda k, f=f: prim_ref[f, k + reach],
-            lambda k: (courant_ref[0, k + reach], courant_ref[1, k + reach]),
+            lambda k: self.prim[f, k + HALO],
+            lambda k: (self.courant[0, k + HALO], self.courant[1, k + HALO]),
         )
+        order = [*range(2, self.count), 0, 1] if self.wrap else range(-1, self.count + 1)
         for k in order:
-            face_ref[0, f, k + reach], face_ref[1, f, k + reach] = faces(k)
-
-    def flux(k, behind=None):
-        before = [face_ref[0, f, k + reach] for f in range(FIELDS)]
-        if behind is None:
-            behind = [face_ref[1, f, k + 1 + reach] for f in range(FIELDS)]
-        return rusanov(before, behind, normal, step)
-
-    def update(k, low, high):
-        old = cons(k)
-        put(k, [old[f] + (low[f] - high[f]) for f in range(FIELDS)])
-
-    if wrap:
-        behind = [next_segment(face_ref[1, f, reach]) for f in range(FIELDS)]
+            self.face[0, f, k + HALO], self.face[1, f, k + HALO] = faces(k)
+
+    def advance(self):
+        count = self.count
+
+        def flux(k, behind=None):
+            before = [self.face[0, f, k + HALO] for f in range(FIELDS)]
+            if behind is None:
+                behind = [self.face[1, f, k + 1 + HALO] for f in range(FIELDS)]
+            return rusanov(before, behind, self.normal, self.step)
+
+        def update(k, low, high):
+            old = self.cons(k)
+            self.put(k, [old[f] + (low[f] - high[f]) for f in range(FIELDS)])
+
+        if not self.wrap:
+            low = flux(-1)
+            for k in range(count):
+                high = flux(k)
+                update(k, low, high)
+                low = high
+            return
+        behind = [next_segment(self.face[1, f, HALO]) for f in range(FIELDS)]
         front = low = flux(0)
-        middle = count // 2
         for k in range(1, count):
-            if k == middle:
+            if k == count // 2:
                 end = flux(count - 1, behind)
                 into = [last_segment(v) for v in end]
             high = flux(k) if k < count - 1 else end
             update(k, low, high)
             low = high
         update(0, into, front)
-        return
-    low = flux(-1)
-    for k in range(count):
-        high = flux(k)
-        update(k, low, high)
-        low = high
+
+
+def in_turn(now, then, beside=None):
+    for f in range(FIELDS):
+        if beside is not None:
+            beside(f)
+        now.rebuild(f)
+    then.ready()
+    now.advance()
 
 
 PEAK_STEPS = 4
@@ -230,52 +244,65 @@
     )(view)
 
 
-def border_kernel(high_ref, low_ref, peak_ref, up_ref, down_ref):
-    up_ref[...] = high_ref[...]
-    down_ref[...] = low_ref[...]
-
-
-def border_call(view, peak):
-    rows = view.shape[1]
-    edge = jax.ShapeDtypeStruct((FIELDS, HALO, 128, 128), jnp.float32)
-    block = (FIELDS, 1, 128, 128)
-    return pl.pallas_call(
-        border_kernel,
-        grid=(HALO,),
-        in_specs=[
-            pl.BlockSpec(block, lambda i: (0, i + rows - HALO, 0, 0)),
-            pl.BlockSpec(block, lambda i: (0, i, 0, 0)),
-            pl.BlockSpec(memory_space=pl.ANY),
-        ],
-        out_specs=[pl.BlockSpec(block, lambda i: (0, i, 0, 0))] * 2,
-        out_shape=[edge, edge],
-        name="border",
-    )(view, view, peak)
-
-
-def turn(turned, slot, f, tile):
+def turn(place_ref, tile):
     flat = tile.T
     for v in range(128 // 8):
         place = (v % 2) * 64 + v // 2
-        turned[slot, f, pl.ds(place, 8, stride=8), :] = flat[v * 8 : (v + 1) * 8]
-
-
-def first_sweep(turned, slot, swept, row, scratch, half, beside):
+        place_ref[pl.ds(place, 8, stride=8), :] = flat[v * 8 : (v + 1) * 8]
+
+
+TURN_STEPS = 4
+
+
+def turn_kernel(state_ref, turned_ref, up_ref, down_ref):
+    rows = state_ref.shape[1]
+    for row in range(rows):
+        for f in range(FIELDS):
+            turn(turned_ref.at[f, row], state_ref[f, row])
+
+    @pl.when(pl.program_id(0) == 0)
+    def _():
+        for row in range(HALO):
+            down_ref[:, row] = turned_ref[:, row]
+
+    @pl.when(pl.program_id(0) == TURN_STEPS - 1)
+    def _():
+        for row in range(HALO):
+            up_ref[:, row] = turned_ref[:, rows - HALO + row]
+
+
+def turn_call(view):
+    edge = (FIELDS, HALO, 128, 128)
+    block = pl.BlockSpec(
+        (FIELDS, view.shape[1] // TURN_STEPS, 128, 128), lambda i: (0, i, 0, 0)
+    )
+    return pl.pallas_call(
+        turn_kernel,
+        grid=(TURN_STEPS,),
+        in_specs=[block],
+        out_specs=[block] + [pl.BlockSpec(edge, lambda i: (0, 0, 0, 0))] * 2,
+        out_shape=[
+            jax.ShapeDtypeStruct(view.shape, jnp.float32),
+            jax.ShapeDtypeStruct(edge, jnp.float32),
+            jax.ShapeDtypeStruct(edge, jnp.float32),
+        ],
+        cost_estimate=pl.CostEstimate(flops=0, bytes_accessed=24 << 20, transcendentals=0),
+        name="turn",
+    )(view)
+
+
+def first_line(turned, row, slot, swept, place, scratch, half):
     def cons(k):
-        return [turned[slot, f, k * 8 : (k + 1) * 8, :] for f in range(FIELDS)]
+        return [turned[f, row, k * 8 : (k + 1) * 8, :] for f in range(FIELDS)]
 
     def put(k, new):
         for f in range(FIELDS):
-            swept[f, row, k] = new[f]
-
-    sweep_line(cons, put, scratch, SEGMENT, 1, half, True, beside)
-
-
-def turn_back(final, row, back, slot, f):
-    final[f, row] = back[slot, f].T
-
-
-def last_sweep(done, row, back, slot, scratch, half, beside):
+            swept[f, place, k] = new[f]
+
+    return Line(cons, put, scratch[slot], SEGMENT, 1, half, True)
+
+
+def last_line(done, row, back, slot, scratch, half):
     def cons(k):
         return [done[f, row, k] for f in range(FIELDS)]
 
@@ -283,10 +310,10 @@
         for f in range(FIELDS):
             back[slot, f, pl.ds(k, 8, stride=SEGMENT), :] = new[f]
 
-    sweep_line(cons, put, scratch, SEGMENT, 1, half, True, beside)
-
-
-def cross_sweep(swept, done, count, row, t, scratch, step):
+    return Line(cons, put, scratch[slot], SEGMENT, 1, half, True)
+
+
+def cross_line(swept, done, count, row, t, slot, scratch, step):
     def cons(k):
         return [swept[f, k + HALO, t] for f in range(FIELDS)]
 
@@ -294,19 +321,27 @@
         for f in range(FIELDS):
             done[f, k + row, t] = new[f]
 
-    sweep_line(cons, put, scratch, count, 2, step, False)
+    return Line(cons, put, scratch[slot], count, 2, step, False)
 
 
 def finish(done, final, back, scratch, half, count, row_out):
+    def line(row, slot):
+        return last_line(done, row, back, slot, scratch, half)
+
+    def turn_back(row, slot):
+        def one(f):
+            final[f, row] = back[slot, f].T
+
+        return one
+
+    line(0, 0).ready()
+
     def two_rows(i, carry):
         row = 2 * i
         earlier = jnp.maximum(row - 1, 0)
-        last_sweep(
-            done, row, back, 0, scratch, half, lambda f: turn_back(final, earlier, back, 1, f)
-        )
-        last_sweep(
-            done, row + 1, back, 1, scratch, half, lambda f: turn_back(final, row, back, 0, f)
-        )
+        later = jnp.minimum(row + 2, count - 1)
+        in_turn(line(row, 0), line(row + 1, 1), turn_back(earlier, 1))
+        in_turn(line(row + 1, 1), line(later, 0), turn_back(row, 0))
 
         @pl.when(i > 0)
         def _():
@@ -317,7 +352,7 @@
 
     lax.fori_loop(0, count // 2, two_rows, 0)
     for f in range(FIELDS):
-        turn_back(final, count - 1, back, 1, f)
+        turn_back(count - 1, 1)(f)
     row_out(count - 1).start()
 
 
@@ -329,11 +364,11 @@
 
 def inner_kernel(
     state_ref, peaks_ref, out_ref, rim_ref,
-    raw, swept, done, final, turned, back, prim, face, courant, in_sems, out_sems, rim_sems,
+    raw, swept, done, final, back, prim, face, courant, in_sems, out_sems, rim_sems,
 ):
     rows = state_ref.shape[1]
     inner = rows - 2 * HALO
-    scratch = (prim, face, courant)
+    scratch = [(prim.at[slot], face, courant.at[slot]) for slot in range(2)]
 
     def row_in(i):
         return pltpu.make_async_copy(state_ref.at[:, i], raw.at[:, i], in_sems.at[i])
@@ -344,9 +379,12 @@
     for i in range(rows):
         row_in(i).start()
     step, half = time_step(peaks_ref)
+
+    def line(row, slot):
+        return first_line(raw, row, slot, swept, row, scratch, half)
+
     row_in(0).wait()
-    for f in range(FIELDS):
-        turn(turned, 0, f, raw[f, 0])
+    line(0, 0).ready()
 
     def two_rows(i, carry):
         row = 2 * i
@@ -357,14 +395,8 @@
         def _():
             row_in(later).wait()
 
-        first_sweep(
-            turned, 0, swept, row, scratch, half,
-            lambda f: turn(turned, 1, f, raw[f, row + 1]),
-        )
-        first_sweep(
-            turned, 1, swept, row + 1, scratch, half,
-            lambda f: turn(turned, 0, f, raw[f, later]),
-        )
+        in_turn(line(row, 0), line(row + 1, 1))
+        in_turn(line(row + 1, 1), line(later, 0))
         return carry
 
     lax.fori_loop(0, rows // 2, two_rows, 0)
@@ -382,11 +414,18 @@
     for copy in rims:
         copy.start()
 
-    def column(t, carry):
-        cross_sweep(swept, done, inner, 0, t, scratch, step)
+    def column(t, slot):
+        return cross_line(swept, done, inner, 0, t, slot, scratch, step)
+
+    column(0, 0).ready()
+
+    def two_columns(i, carry):
+        t = 2 * i
+        in_turn(column(t, 0), column(t + 1, 1))
+        in_turn(column(t + 1, 1), column(jnp.minimum(t + 2, SEGMENT - 1), 0))
         return carry
 
-    lax.fori_loop(0, SEGMENT, column, 0)
+    lax.fori_loop(0, SEGMENT // 2, two_columns, 0)
     finish(done, final, back, scratch, half, inner, row_out)
     for copy in rims:
         copy.wait()
@@ -396,10 +435,10 @@
 
 def outer_kernel(
     rim_ref, low_ref, high_ref, peaks_ref, half_done_ref, out_ref,
-    raw, lower, upper, done, final, turned, back, prim, face, courant, in_sems, out_sems,
+    raw, lower, upper, done, final, back, prim, face, courant, in_sems, out_sems,
 ):
     rows = out_ref.shape[1]
-    scratch = (prim, face, courant)
+    scratch = [(prim.at[slot], face, courant.at[slot]) for slot in range(2)]
     copies = (
         pltpu.make_async_copy(low_ref, raw.at[:, pl.ds(0, HALO)], in_sems.at[0]),
         pltpu.make_async_copy(high_ref, raw.at[:, pl.ds(HALO, HALO)], in_sems.at[1]),
@@ -419,29 +458,36 @@
         copy.start()
     step, half = time_step(peaks_ref)
     copies[0].wait()
-    for f in range(FIELDS):
-        turn(turned, 0, f, raw[f, 0])
     copies[1].wait()
 
+    def low_line(row):
+        return first_line(raw, row, 0, lower, row, scratch, half)
+
+    def high_line(row):
+        return first_line(raw, row + HALO, 1, upper, row + 2 * HALO, scratch, half)
+
+    low_line(0).ready()
+
     def two_rows(i, carry):
-        later = jnp.minimum(i + 1, HALO - 1)
-        first_sweep(
-            turned, 0, lower, i, scratch, half,
-            lambda f: turn(turned, 1, f, raw[f, i + HALO]),
-        )
-        first_sweep(
-            turned, 1, upper, i + 2 * HALO, scratch, half,
-            lambda f: turn(turned, 0, f, raw[f, later]),
-        )
+        in_turn(low_line(i), high_line(i))
+        in_turn(high_line(i), low_line(jnp.minimum(i + 1, HALO - 1)))
         return carry
 
     lax.fori_loop(0, HALO, two_rows, 0)
     copies[2].wait()
     copies[3].wait()
 
+    def low_column(t):
+        return cross_line(lower, done, HALO, 0, t, 0, scratch, step)
+
+    def high_column(t):
+        return cross_line(upper, done, HALO, HALO, t, 1, scratch, step)
+
+    low_column(0).ready()
+
     def column(t, carry):
-        cross_sweep(lower, done, HALO, 0, t, scratch, step)
-        cross_sweep(upper, done, HALO, HALO, t, scratch, step)
+        in_turn(low_column(t), high_column(t))
+        in_turn(high_column(t), low_column(jnp.minimum(t + 1, SEGMENT - 1)))
         return carry
 
     lax.fori_loop(0, SEGMENT, column, 0)
@@ -453,10 +499,9 @@
 def line_scratch(length):
     return [
         pltpu.VMEM((2, FIELDS, 128, 128), jnp.float32),
-        pltpu.VMEM((2, FIELDS, 128, 128), jnp.float32),
-        pltpu.VMEM((FIELDS, length + 2 * HALO, 8, 128), jnp.float32),
         pltpu.VMEM((2, FIELDS, length + 2 * HALO, 8, 128), jnp.float32),
-        pltpu.VMEM((2, length + 2 * HALO, 8, 128), jnp.float32),
+        pltpu.VMEM((2, FIELDS, length + 2 * HALO, 8, 128), jnp.float32),
+        pltpu.VMEM((2, 2, length + 2 * HALO, 8, 128), jnp.float32),
     ]
 
 
@@ -521,10 +566,10 @@
     up = [(i, (i + 1) % devices) for i in range(devices)]
     peak = peak_call(view, devices)
     peaks = lax.all_to_all(peak, WIDE_NARROW, 0, 0, tiled=True)
-    send_up, send_down = border_call(view, peaks)
+    peaks, turned, send_up, send_down = lax.optimization_barrier((peaks, *turn_call(view)))
     low = lax.ppermute(send_up, WIDE_NARROW, up)
     high = lax.ppermute(send_down, WIDE_NARROW, [(b, a) for a, b in up])
-    out, rim = inner_call(view, peaks)
+    out, rim = inner_call(turned, peaks)
     out = outer_call(rim, low, high, peaks, out)
     out = out.reshape(fields, rows, tiles, planes, 128).transpose(0, 1, 3, 2, 4)
     return out.reshape(fields, rows, planes, columns)

time: 75.5 us -> 68.9 us (0.913)
  blocking collectives: 20.9 us -> 0 us
  starting transfers between devices: 7.18 us -> 18.3 us
  waiting for transfers between devices: 0.01 us -> 2.5 us
    all_to_all x1 -> x0, blocking collectives: 20.9 us -> none  [local(): peaks = lax.all_to_all(peak, WIDE_NARROW, 0, 0, tiled=True)]
    all_to_all x0 -> x1, starting transfers between devices: none -> 11.1 us  [local(): peaks = lax.all_to_all(peak, WIDE_NARROW, 0, 0, tiled=True)]
    pallas_call x1, Pallas kernels: 3.65 us -> 6.69 us  [turn_call(): pl.pallas_call(turn_kernel, grid=(TURN_STEPS,), in_specs=[block], out_spe...]
    all_to_all x0 -> x1, waiting for transfers between devices: none -> 2.5 us  [local(): peaks = lax.all_to_all(peak, WIDE_NARROW, 0, 0, tiled=True)]
    pallas_call x1, Pallas kernels: 24.7 us -> 23 us  [inner_call(): pl.pallas_call(inner_kernel, in_specs=[anywhere, pl.BlockSpec(memory_spac...]
  transfers between devices with their start and end apart: 2 -> 3, of which waited for: 0 -> 1; matrix products, arithmetic and copies ran while one was open for 0% -> 0% of each run, Pallas kernels for 33% -> 43%
where the time goes in v3:
time: 68.9 us; the launch traced here: 68.6 us
  Pallas kernels  47.7 us (69%)
  starting transfers between devices  18.3 us (27%)
  waiting for transfers between devices  2.5 us (4%)
    pallas_call x1, Pallas kernels, inner_call(): pl.pallas_call(inner_kernel, in_specs=[anywhere, pl.BlockSpec(memory_spac...  23 us
    pallas_call x1, Pallas kernels, outer_call(): pl.pallas_call(outer_kernel, in_specs=[anywhere, anywhere, anywhere, pl.B...  13.7 us
    all_to_all x1, starting transfers between devices, local(): peaks = lax.all_to_all(peak, WIDE_NARROW, 0, 0, tiled=True)  11.1 us
    pallas_call x1, Pallas kernels, turn_call(): pl.pallas_call(turn_kernel, grid=(TURN_STEPS,), in_specs=[block], out_spe...  6.69 us
    ppermute x1, starting transfers between devices, local(): high = lax.ppermute(send_down, WIDE_NARROW, [(b, a) for a, b in up])  6.34 us
    pallas_call x1, Pallas kernels, peak_call(): pl.pallas_call(peak_kernel, grid=(PEAK_STEPS,), in_specs=[pl.BlockSpec((F...  4.38 us
    all_to_all x1, waiting for transfers between devices, local(): peaks = lax.all_to_all(peak, WIDE_NARROW, 0, 0, tiled=True)  2.5 us
  transfers between devices with their start and end apart: 3, of which 1 were waited for; matrix products, arithmetic and copies ran while one was open for 0% of the time, Pallas kernels for 43%

profile of v3, /device:TPU:0, one launch (start us, length us, event | category | flops | bytes accessed | tf_op | source)
XLA Modules:
  0.0 68.6 jit_solution(632555940517489345)
XLA Ops:
  0.0 4.4 %peak.1 = f32[128,128]{1,0:T(8,128)} custom-call(f32[5,16,128,128]{3,2,1,0:T(8,128)} %bitcast.16), custom_call_target="tpu_custom_call" | custom-call | tf_op jit(solution)/shard_map/peak/pallas_call | solution.py:236
  4.4 11.1 %all-to-all-start = ((f32[128,1,128]{2,1,0:T(1,128)}), f32[128,1,128]{2,1,0:T(1,128)S(1)}, u32[]{:S(2)}, u32[]{:S(2)}) async-start(f32[128,1,128]{2,1,0:T(1,128)} %bitcast.18), calls=%async_computation | async-start | bytes 131072 | tf_op jit(solution)/shard_map/all_to_all | solution.py:568
  15.5 6.7 %turn.1 = (f32[5,16,128,128]{3,2,1,0:T(8,128)}, f32[5,3,128,128]{3,2,1,0:T(8,128)}, f32[5,3,128,128]{3,2,1,0:T(8,128)}) custom-call(f32[5,16,128,128]{3,2,1,0:T(8,128)} %bitcast.17), custom_call_target="tpu_custom_call" | custom-call | bytes 25165824 | tf_op jit(solution)/shard_map/turn/pallas_call | solution.py:279
  22.2 2.5 %all-to-all-done = f32[128,1,128]{2,1,0:T(1,128)S(1)} async-done(((f32[128,1,128]{2,1,0:T(1,128)}), f32[128,1,128]{2,1,0:T(1,128)S(1)}, u32[]{:S(2)}, u32[]{:S(2)}) %all-to-all-start) | async-done | bytes 65568 | tf_op jit(solution)/shard_map/all_to_all | solution.py:568
  24.7 0.8 %collective-permute-start = (f32[5,3,128,128]{3,2,1,0:T(8,128)}, f32[5,3,128,128]{3,2,1,0:T(8,128)S(1)}, u32[]{:S(2)}, u32[]{:S(2)}) collective-permute-start(f32[5,3,128,128]{3,2,1,0:T(8,128)} %get-tuple-element.20), channel_id=1, source_target_pairs={{0,1},{1,2},{2,3},{3,4},{4,5},{5,6},{6,7},{7,8},{8,9},{9,10},{10,1... | collective-permute-start | bytes 2949128 | tf_op jit(solution)/shard_map/ppermute | solution.py:570
  25.6 6.3 %collective-permute-start.1 = (f32[5,3,128,128]{3,2,1,0:T(8,128)}, f32[5,3,128,128]{3,2,1,0:T(8,128)S(1)}, u32[]{:S(2)}, u32[]{:S(2)}) collective-permute-start(f32[5,3,128,128]{3,2,1,0:T(8,128)} %get-tuple-element.21), channel_id=1, source_target_pairs={{1,0},{2,1},{3,2},{4,3},{5,4},{6,5},{7,6},{8,7},{9,8},{10,9},{11,1... | collective-permute-start | bytes 2949128 | tf_op jit(solution)/shard_map/ppermute | solution.py:571
  31.9 23.0 %inner.1 = (f32[5,16,128,128]{3,2,1,0:T(8,128)}, f32[5,12,16,8,128]{4,3,2,1,0:T(8,128)S(1)}) custom-call(f32[5,16,128,128]{3,2,1,0:T(8,128)} %get-tuple-element.17.state_ref, f32[128,128]{1,0:T(8,128)S(1)} %bitcast.14), custom_call_target="tpu_custom_call" | custom-call | tf_op jit(solution)/shard_map/inner/pallas_call | solution.py:512
  54.9 0.0 collective-permute-done.low_ref
  54.9 0.0 collective-permute-done.1.high_ref
  54.9 13.7 %outer.1 = f32[5,16,128,128]{3,2,1,0:T(8,128)} custom-call(f32[5,12,16,8,128]{4,3,2,1,0:T(8,128)S(1)} %get-tuple-element.19.rim_ref, f32[5,3,128,128]{3,2,1,0:T(8,128)S(1)} %collective-permute-done.low_ref, f32[5,3,128,128]{3,2,1,0:T(8,128)S(1)} %collective-permute-done.1.high_ref, f32[128,128]{1,0:T(8,128)S(1)} %bitcast.15, ...), custom_call_target="tpu_custom_call", output_to_operand_aliasing={{}: (4, {})} | custom-call | tf_op jit(solution)/shard_map/outer/pallas_call | solution.py:537
Async XLA Ops:
  4.4 20.3 %all-to-all-start = ((f32[128,1,128]{2,1,0:T(1,128)}), f32[128,1,128]{2,1,0:T(1,128)S(1)}, u32[]{:S(2)}, u32[]{:S(2)}) async-start(f32[128,1,128]{2,1,0:T(1,128)} %bitcast.18), calls=%async_computation | async-start | bytes 131072 | tf_op jit(solution)/shard_map/all_to_all | solution.py:568
  24.7 30.2 %collective-permute-start = (f32[5,3,128,128]{3,2,1,0:T(8,128)}, f32[5,3,128,128]{3,2,1,0:T(8,128)S(1)}, u32[]{:S(2)}, u32[]{:S(2)}) collective-permute-start(f32[5,3,128,128]{3,2,1,0:T(8,128)} %get-tuple-element.20), channel_id=1, source_target_pairs={{0,1},{1,2},{2,3},{3,4},{4,5},{5,6},{6,7},{7,8},{8,9},{9,10},{10,1... | collective-permute-start | bytes 2949128 | tf_op jit(solution)/shard_map/ppermute | solution.py:570
  25.6 29.4 %collective-permute-start.1 = (f32[5,3,128,128]{3,2,1,0:T(8,128)}, f32[5,3,128,128]{3,2,1,0:T(8,128)S(1)}, u32[]{:S(2)}, u32[]{:S(2)}) collective-permute-start(f32[5,3,128,128]{3,2,1,0:T(8,128)} %get-tuple-element.21), channel_id=1, source_target_pairs={{1,0},{2,1},{3,2},{4,3},{5,4},{6,5},{7,6},{8,7},{9,8},{10,9},{11,1... | collective-permute-start | bytes 2949128 | tf_op jit(solution)/shard_map/ppermute | solution.py:571

commit v4 on v3

--- a/solution.py
+++ b/solution.py
@@ -195,51 +195,47 @@
     now.advance()
 
 
-PEAK_STEPS = 4
-
-
-def peak_kernel(state_ref, peak_ref, best_ref):
-    rows = state_ref.shape[1]
-    place = pl.program_id(0)
-
-    def body(i, best):
+PEAK_ROWS = 2
+
+
+def peak_kernel(state_ref, peak_ref, raw, sems):
+    parts = state_ref.shape[1] // PEAK_ROWS
+
+    def part_in(i):
+        rows = pl.ds(i * PEAK_ROWS, PEAK_ROWS)
+        return pltpu.make_async_copy(state_ref.at[:, rows], raw.at[:, rows], sems.at[i])
+
+    for i in range(parts):
+        part_in(i).start()
+
+    def one_part(i, best):
+        part_in(i).wait()
         best = list(best)
-        for row in range(rows):
-            at = pl.ds(pl.multiple_of(i * 8, 8), 8)
-            prim = primitives([state_ref[f, row, at, :] for f in range(FIELDS)])
-            sound = sound_speed(prim[0], prim[4])
-            new = jnp.maximum(jnp.abs(prim[1]), jnp.abs(prim[2])) + sound
-            best[row] = jnp.maximum(best[row], new)
+        for row in range(PEAK_ROWS):
+            for k in range(16):
+                at = slice(k * 8, (k + 1) * 8)
+                prim = primitives([raw[f, i * PEAK_ROWS + row, at, :] for f in range(FIELDS)])
+                sound = sound_speed(prim[0], prim[4])
+                new = jnp.maximum(jnp.abs(prim[1]), jnp.abs(prim[2])) + sound
+                best[k % 4] = jnp.maximum(best[k % 4], new)
         return tuple(best)
 
     zero = jnp.zeros((8, 128), jnp.float32)
-    parts = lax.fori_loop(0, 16, body, (zero,) * rows, unroll=4)
-    best = parts[0]
-    for part in parts[1:]:
-        best = jnp.maximum(best, part)
-
-    @pl.when(place == 0)
-    def _():
-        best_ref[...] = best
-
-    @pl.when(place > 0)
-    def _():
-        best_ref[...] = jnp.maximum(best_ref[...], best)
-
-    @pl.when(place == PEAK_STEPS - 1)
-    def _():
-        peak_ref[...] = jnp.full(peak_ref.shape, jnp.max(best_ref[...]), jnp.float32)
+    best = lax.fori_loop(0, parts, one_part, (zero,) * 4)
+    best = jnp.maximum(jnp.maximum(best[0], best[1]), jnp.maximum(best[2], best[3]))
+    peak_ref[...] = jnp.full(peak_ref.shape, jnp.max(best), jnp.float32)
 
 
 def peak_call(view, devices):
-    rows = view.shape[1]
     return pl.pallas_call(
         peak_kernel,
-        grid=(PEAK_STEPS,),
-        in_specs=[pl.BlockSpec((FIELDS, rows // PEAK_STEPS, 128, 128), lambda i: (0, i, 0, 0))],
-        out_specs=pl.BlockSpec((devices, 128), lambda i: (0, 0)),
+        in_specs=[pl.BlockSpec(memory_space=pl.ANY)],
+        out_specs=pl.BlockSpec(memory_space=pltpu.VMEM),
         out_shape=jax.ShapeDtypeStruct((devices, 128), jnp.float32),
-        scratch_shapes=[pltpu.VMEM((8, 128), jnp.float32)],
+        scratch_shapes=[
+            pltpu.VMEM(view.shape, jnp.float32),
+            pltpu.SemaphoreType.DMA((view.shape[1] // PEAK_ROWS,)),
+        ],
         name="peak",
     )(view)
 
@@ -485,12 +481,15 @@
 
     low_column(0).ready()
 
-    def column(t, carry):
+    def two_columns(i, carry):
+        t = 2 * i
         in_turn(low_column(t), high_column(t))
-        in_turn(high_column(t), low_column(jnp.minimum(t + 1, SEGMENT - 1)))
+        in_turn(high_column(t), low_column(t + 1))
+        in_turn(low_column(t + 1), high_column(t + 1))
+        in_turn(high_column(t + 1), low_column(jnp.minimum(t + 2, SEGMENT - 1)))
         return carry
 
-    lax.fori_loop(0, SEGMENT, column, 0)
+    lax.fori_loop(0, SEGMENT // 2, two_columns, 0)
     finish(done, final, back, scratch, half, 2 * HALO, row_out)
     for i in range(2 * HALO):
         row_out(i).wait()

time: 68.9 us -> 67.7 us (0.983)
  Pallas kernels: 47.7 us -> 46.7 us
    pallas_call x1, Pallas kernels: 4.38 us -> 3.39 us  [peak_call(): pl.pallas_call(peak_kernel, in_specs=[pl.BlockSpec(memory_space=pl.ANY)],...]
  transfers between devices with their start and end apart: 3 -> 3, of which waited for: 1 -> 1; matrix products, arithmetic and copies ran while one was open for 0% -> 0% of each run, Pallas kernels for 43% -> 44%
where the time goes in v4:
time: 67.7 us; the launch traced here: 67.5 us
  Pallas kernels  46.7 us (69%)
  starting transfers between devices  18.3 us (27%)
  waiting for transfers between devices  2.5 us (4%)
    pallas_call x1, Pallas kernels, inner_call(): pl.pallas_call(inner_kernel, in_specs=[anywhere, pl.BlockSpec(memory_spac...  23 us
    pallas_call x1, Pallas kernels, outer_call(): pl.pallas_call(outer_kernel, in_specs=[anywhere, anywhere, anywhere, pl.B...  13.6 us
    all_to_all x1, starting transfers between devices, local(): peaks = lax.all_to_all(peak, WIDE_NARROW, 0, 0, tiled=True)  11.1 us
    pallas_call x1, Pallas kernels, turn_call(): pl.pallas_call(turn_kernel, grid=(TURN_STEPS,), in_specs=[block], out_spe...  6.69 us
    ppermute x1, starting transfers between devices, local(): high = lax.ppermute(send_down, WIDE_NARROW, [(b, a) for a, b in up])  6.34 us
    pallas_call x1, Pallas kernels, peak_call(): pl.pallas_call(peak_kernel, in_specs=[pl.BlockSpec(memory_space=pl.ANY)],...  3.39 us
    all_to_all x1, waiting for transfers between devices, local(): peaks = lax.all_to_all(peak, WIDE_NARROW, 0, 0, tiled=True)  2.5 us
  transfers between devices with their start and end apart: 3, of which 1 were waited for; matrix products, arithmetic and copies ran while one was open for 0% of the time, Pallas kernels for 44%

profile of v4, /device:TPU:0, one launch (start us, length us, event | category | flops | bytes accessed | tf_op | source)
XLA Modules:
  0.0 67.5 jit_solution(11981199030979697435)
XLA Ops:
  0.0 3.4 %peak.1 = f32[128,128]{1,0:T(8,128)} custom-call(f32[5,16,128,128]{3,2,1,0:T(8,128)} %bitcast.16), custom_call_target="tpu_custom_call" | custom-call | tf_op jit(solution)/shard_map/peak/pallas_call | solution.py:230
  3.4 11.1 %all-to-all-start = ((f32[128,1,128]{2,1,0:T(1,128)}), f32[128,1,128]{2,1,0:T(1,128)S(1)}, u32[]{:S(2)}, u32[]{:S(2)}) async-start(f32[128,1,128]{2,1,0:T(1,128)} %bitcast.18), calls=%async_computation | async-start | bytes 131072 | tf_op jit(solution)/shard_map/all_to_all | solution.py:567
  14.6 6.7 %turn.1 = (f32[5,16,128,128]{3,2,1,0:T(8,128)}, f32[5,3,128,128]{3,2,1,0:T(8,128)}, f32[5,3,128,128]{3,2,1,0:T(8,128)}) custom-call(f32[5,16,128,128]{3,2,1,0:T(8,128)} %bitcast.17), custom_call_target="tpu_custom_call" | custom-call | bytes 25165824 | tf_op jit(solution)/shard_map/turn/pallas_call | solution.py:275
  21.2 2.5 %all-to-all-done = f32[128,1,128]{2,1,0:T(1,128)S(1)} async-done(((f32[128,1,128]{2,1,0:T(1,128)}), f32[128,1,128]{2,1,0:T(1,128)S(1)}, u32[]{:S(2)}, u32[]{:S(2)}) %all-to-all-start) | async-done | bytes 65568 | tf_op jit(solution)/shard_map/all_to_all | solution.py:567
  23.7 0.8 %collective-permute-start = (f32[5,3,128,128]{3,2,1,0:T(8,128)}, f32[5,3,128,128]{3,2,1,0:T(8,128)S(1)}, u32[]{:S(2)}, u32[]{:S(2)}) collective-permute-start(f32[5,3,128,128]{3,2,1,0:T(8,128)} %get-tuple-element.20), channel_id=1, source_target_pairs={{0,1},{1,2},{2,3},{3,4},{4,5},{5,6},{6,7},{7,8},{8,9},{9,10},{10,1... | collective-permute-start | bytes 2949128 | tf_op jit(solution)/shard_map/ppermute | solution.py:569
  24.6 6.3 %collective-permute-start.1 = (f32[5,3,128,128]{3,2,1,0:T(8,128)}, f32[5,3,128,128]{3,2,1,0:T(8,128)S(1)}, u32[]{:S(2)}, u32[]{:S(2)}) collective-permute-start(f32[5,3,128,128]{3,2,1,0:T(8,128)} %get-tuple-element.21), channel_id=1, source_target_pairs={{1,0},{2,1},{3,2},{4,3},{5,4},{6,5},{7,6},{8,7},{9,8},{10,9},{11,1... | collective-permute-start | bytes 2949128 | tf_op jit(solution)/shard_map/ppermute | solution.py:570
  30.9 23.0 %inner.1 = (f32[5,16,128,128]{3,2,1,0:T(8,128)}, f32[5,12,16,8,128]{4,3,2,1,0:T(8,128)S(1)}) custom-call(f32[5,16,128,128]{3,2,1,0:T(8,128)} %get-tuple-element.17.state_ref, f32[128,128]{1,0:T(8,128)S(1)} %bitcast.14), custom_call_target="tpu_custom_call" | custom-call | tf_op jit(solution)/shard_map/inner/pallas_call | solution.py:511
  53.9 0.0 collective-permute-done.low_ref
  53.9 0.0 collective-permute-done.1.high_ref
  54.0 13.6 %outer.1 = f32[5,16,128,128]{3,2,1,0:T(8,128)} custom-call(f32[5,12,16,8,128]{4,3,2,1,0:T(8,128)S(1)} %get-tuple-element.19.rim_ref, f32[5,3,128,128]{3,2,1,0:T(8,128)S(1)} %collective-permute-done.low_ref, f32[5,3,128,128]{3,2,1,0:T(8,128)S(1)} %collective-permute-done.1.high_ref, f32[128,128]{1,0:T(8,128)S(1)} %bitcast.15, ...), custom_call_target="tpu_custom_call", output_to_operand_aliasing={{}: (4, {})} | custom-call | tf_op jit(solution)/shard_map/outer/pallas_call | solution.py:536
Async XLA Ops:
  3.4 20.3 %all-to-all-start = ((f32[128,1,128]{2,1,0:T(1,128)}), f32[128,1,128]{2,1,0:T(1,128)S(1)}, u32[]{:S(2)}, u32[]{:S(2)}) async-start(f32[128,1,128]{2,1,0:T(1,128)} %bitcast.18), calls=%async_computation | async-start | bytes 131072 | tf_op jit(solution)/shard_map/all_to_all | solution.py:567
  23.7 30.2 %collective-permute-start = (f32[5,3,128,128]{3,2,1,0:T(8,128)}, f32[5,3,128,128]{3,2,1,0:T(8,128)S(1)}, u32[]{:S(2)}, u32[]{:S(2)}) collective-permute-start(f32[5,3,128,128]{3,2,1,0:T(8,128)} %get-tuple-element.20), channel_id=1, source_target_pairs={{0,1},{1,2},{2,3},{3,4},{4,5},{5,6},{6,7},{7,8},{8,9},{9,10},{10,1... | collective-permute-start | bytes 2949128 | tf_op jit(solution)/shard_map/ppermute | solution.py:569
  24.6 29.4 %collective-permute-start.1 = (f32[5,3,128,128]{3,2,1,0:T(8,128)}, f32[5,3,128,128]{3,2,1,0:T(8,128)S(1)}, u32[]{:S(2)}, u32[]{:S(2)}) collective-permute-start(f32[5,3,128,128]{3,2,1,0:T(8,128)} %get-tuple-element.21), channel_id=1, source_target_pairs={{1,0},{2,1},{3,2},{4,3},{5,4},{6,5},{7,6},{8,7},{9,8},{10,9},{11,1... | collective-permute-start | bytes 2949128 | tf_op jit(solution)/shard_map/ppermute | solution.py:570

commit v5 on v4

--- a/solution.py
+++ b/solution.py
@@ -55,12 +55,16 @@
         return value
 
 
-def make_reconstruct(cell, courant):
+def make_reconstruct(cell, courant, closed=None):
     def jump(k):
         step = cells[k + 1] - cells[k]
         return jnp.abs(step), step > 0
 
     def slope(k):
+        if closed is not None and k == -1:
+            return last_segment(slopes[closed - 1][0]), None
+        if closed is not None and k == closed:
+            return next_segment(slopes[0][0]), None
         (back, back_up), (fore, fore_up) = jumps[k - 1], jumps[k]
         turns = jnp.logical_xor(back_up, fore_up)
         size = jnp.minimum(back + fore, 4.0 * jnp.minimum(back, fore))
@@ -81,6 +85,8 @@
         return base + right, base - left
 
     cells, jumps, slopes, edges = Lazy(cell), Lazy(jump), Lazy(slope), Lazy(edge)
+    if closed is not None:
+        slopes[closed], slopes[-1]
     return faces
 
 
@@ -134,21 +140,20 @@
             for k in range(-HALO, count + HALO):
                 start(k)
             return
-        for k in (0, 1):
-            prim = start(k)
-            for f in range(FIELDS):
-                self.prim[f, count + k + HALO] = next_segment(prim[f])
-        for k in (count - 2, count - 1):
-            prim = start(k)
-            for f in range(FIELDS):
-                self.prim[f, k - count + HALO] = last_segment(prim[f])
-        for k in range(2, count - 2):
+        prim = start(0)
+        for f in range(FIELDS):
+            self.prim[f, count + HALO] = next_segment(prim[f])
+        prim = start(count - 1)
+        for f in range(FIELDS):
+            self.prim[f, HALO - 1] = last_segment(prim[f])
+        for k in range(1, count - 1):
             start(k)
 
     def rebuild(self, f):
         faces = make_reconstruct(
             lambda k: self.prim[f, k + HALO],
             lambda k: (self.courant[0, k + HALO], self.courant[1, k + HALO]),
+            self.count if self.wrap else None,
         )
         order = [*range(2, self.count), 0, 1] if self.wrap else range(-1, self.count + 1)
         for k in order:

time: 67.7 us -> 67 us (0.990)
  Pallas kernels: 46.7 us -> 45.9 us
where the time goes in v5:
time: 67 us; the launch traced here: 66.8 us
  Pallas kernels  45.9 us (69%)
  starting transfers between devices  18.3 us (27%)
  waiting for transfers between devices  2.5 us (4%)
    pallas_call x1, Pallas kernels, inner_call(): pl.pallas_call(inner_kernel, in_specs=[anywhere, pl.BlockSpec(memory_spac...  22.5 us
    pallas_call x1, Pallas kernels, outer_call(): pl.pallas_call(outer_kernel, in_specs=[anywhere, anywhere, anywhere, pl.B...  13.3 us
    all_to_all x1, starting transfers between devices, local(): peaks = lax.all_to_all(peak, WIDE_NARROW, 0, 0, tiled=True)  11.1 us
    pallas_call x1, Pallas kernels, turn_call(): pl.pallas_call(turn_kernel, grid=(TURN_STEPS,), in_specs=[block], out_spe...  6.69 us
    ppermute x1, starting transfers between devices, local(): high = lax.ppermute(send_down, WIDE_NARROW, [(b, a) for a, b in up])  6.34 us
    pallas_call x1, Pallas kernels, peak_call(): pl.pallas_call(peak_kernel, in_specs=[pl.BlockSpec(memory_space=pl.ANY)],...  3.39 us
    all_to_all x1, waiting for transfers between devices, local(): peaks = lax.all_to_all(peak, WIDE_NARROW, 0, 0, tiled=True)  2.5 us
  transfers between devices with their start and end apart: 3, of which 1 were waited for; matrix products, arithmetic and copies ran while one was open for 0% of the time, Pallas kernels for 44%

profile of v5, /device:TPU:0, one launch (start us, length us, event | category | flops | bytes accessed | tf_op | source)
XLA Modules:
  0.0 66.8 jit_solution(2642010412109692393)
XLA Ops:
  0.0 3.4 %peak.1 = f32[128,128]{1,0:T(8,128)} custom-call(f32[5,16,128,128]{3,2,1,0:T(8,128)} %bitcast.16), custom_call_target="tpu_custom_call" | custom-call | tf_op jit(solution)/shard_map/peak/pallas_call | solution.py:235
  3.4 11.1 %all-to-all-start = ((f32[128,1,128]{2,1,0:T(1,128)}), f32[128,1,128]{2,1,0:T(1,128)S(1)}, u32[]{:S(2)}, u32[]{:S(2)}) async-start(f32[128,1,128]{2,1,0:T(1,128)} %bitcast.18), calls=%async_computation | async-start | bytes 131072 | tf_op jit(solution)/shard_map/all_to_all | solution.py:572
  14.6 6.7 %turn.1 = (f32[5,16,128,128]{3,2,1,0:T(8,128)}, f32[5,3,128,128]{3,2,1,0:T(8,128)}, f32[5,3,128,128]{3,2,1,0:T(8,128)}) custom-call(f32[5,16,128,128]{3,2,1,0:T(8,128)} %bitcast.17), custom_call_target="tpu_custom_call" | custom-call | bytes 25165824 | tf_op jit(solution)/shard_map/turn/pallas_call | solution.py:280
  21.2 2.5 %all-to-all-done = f32[128,1,128]{2,1,0:T(1,128)S(1)} async-done(((f32[128,1,128]{2,1,0:T(1,128)}), f32[128,1,128]{2,1,0:T(1,128)S(1)}, u32[]{:S(2)}, u32[]{:S(2)}) %all-to-all-start) | async-done | bytes 65568 | tf_op jit(solution)/shard_map/all_to_all | solution.py:572
  23.7 0.8 %collective-permute-start = (f32[5,3,128,128]{3,2,1,0:T(8,128)}, f32[5,3,128,128]{3,2,1,0:T(8,128)S(1)}, u32[]{:S(2)}, u32[]{:S(2)}) collective-permute-start(f32[5,3,128,128]{3,2,1,0:T(8,128)} %get-tuple-element.20), channel_id=1, source_target_pairs={{0,1},{1,2},{2,3},{3,4},{4,5},{5,6},{6,7},{7,8},{8,9},{9,10},{10,1... | collective-permute-start | bytes 2949128 | tf_op jit(solution)/shard_map/ppermute | solution.py:574
  24.6 6.3 %collective-permute-start.1 = (f32[5,3,128,128]{3,2,1,0:T(8,128)}, f32[5,3,128,128]{3,2,1,0:T(8,128)S(1)}, u32[]{:S(2)}, u32[]{:S(2)}) collective-permute-start(f32[5,3,128,128]{3,2,1,0:T(8,128)} %get-tuple-element.21), channel_id=1, source_target_pairs={{1,0},{2,1},{3,2},{4,3},{5,4},{6,5},{7,6},{8,7},{9,8},{10,9},{11,1... | collective-permute-start | bytes 2949128 | tf_op jit(solution)/shard_map/ppermute | solution.py:575
  30.9 22.5 %inner.1 = (f32[5,16,128,128]{3,2,1,0:T(8,128)}, f32[5,12,16,8,128]{4,3,2,1,0:T(8,128)S(1)}) custom-call(f32[5,16,128,128]{3,2,1,0:T(8,128)} %get-tuple-element.17.state_ref, f32[128,128]{1,0:T(8,128)S(1)} %bitcast.14), custom_call_target="tpu_custom_call" | custom-call | tf_op jit(solution)/shard_map/inner/pallas_call | solution.py:516
  53.5 0.0 collective-permute-done.low_ref
  53.5 0.0 collective-permute-done.1.high_ref
  53.5 13.3 %outer.1 = f32[5,16,128,128]{3,2,1,0:T(8,128)} custom-call(f32[5,12,16,8,128]{4,3,2,1,0:T(8,128)S(1)} %get-tuple-element.19.rim_ref, f32[5,3,128,128]{3,2,1,0:T(8,128)S(1)} %collective-permute-done.low_ref, f32[5,3,128,128]{3,2,1,0:T(8,128)S(1)} %collective-permute-done.1.high_ref, f32[128,128]{1,0:T(8,128)S(1)} %bitcast.15, ...), custom_call_target="tpu_custom_call", output_to_operand_aliasing={{}: (4, {})} | custom-call | tf_op jit(solution)/shard_map/outer/pallas_call | solution.py:541
Async XLA Ops:
  3.4 20.3 %all-to-all-start = ((f32[128,1,128]{2,1,0:T(1,128)}), f32[128,1,128]{2,1,0:T(1,128)S(1)}, u32[]{:S(2)}, u32[]{:S(2)}) async-start(f32[128,1,128]{2,1,0:T(1,128)} %bitcast.18), calls=%async_computation | async-start | bytes 131072 | tf_op jit(solution)/shard_map/all_to_all | solution.py:572
  23.7 29.7 %collective-permute-start = (f32[5,3,128,128]{3,2,1,0:T(8,128)}, f32[5,3,128,128]{3,2,1,0:T(8,128)S(1)}, u32[]{:S(2)}, u32[]{:S(2)}) collective-permute-start(f32[5,3,128,128]{3,2,1,0:T(8,128)} %get-tuple-element.20), channel_id=1, source_target_pairs={{0,1},{1,2},{2,3},{3,4},{4,5},{5,6},{6,7},{7,8},{8,9},{9,10},{10,1... | collective-permute-start | bytes 2949128 | tf_op jit(solution)/shard_map/ppermute | solution.py:574
  24.6 28.9 %collective-permute-start.1 = (f32[5,3,128,128]{3,2,1,0:T(8,128)}, f32[5,3,128,128]{3,2,1,0:T(8,128)S(1)}, u32[]{:S(2)}, u32[]{:S(2)}) collective-permute-start(f32[5,3,128,128]{3,2,1,0:T(8,128)} %get-tuple-element.21), channel_id=1, source_target_pairs={{1,0},{2,1},{3,2},{4,3},{5,4},{6,5},{7,6},{8,7},{9,8},{10,9},{11,1... | collective-permute-start | bytes 2949128 | tf_op jit(solution)/shard_map/ppermute | solution.py:575
